TPU v7x, 256 devices: a whole 4x4x8 slice. The times are simulated.
256 devices in a mesh: dp: 32 (over z, y), mp: 8 (over x, core).
Axes of the slice: x: 4, y: 4, z: 8, core: 2. Of those that a mesh axis runs over, the one named last changes fastest.
Arguments:
- tokens: bfloat16 [12288, 4096], P(('dp', 'mp')), may hold values from -8 to 8
- encoded: bfloat16 [128, 128, 1024], P('dp'), may hold values from -8 to 8
- neighbour_owner: int32 [32, 6, 2], replicated, may hold values from 0 to 31, as said below
- neighbour_slot: int32 [32, 6, 2], replicated, may hold values from 0 to 3
- w_query: bfloat16 [4096, 4096], P(None, 'mp'), may hold values from -0.09375 to 0.09375
- w_key: bfloat16 [1024, 4096], P(None, 'mp'), may hold values from -0.1875 to 0.1875
- w_value: bfloat16 [1024, 4096], P(None, 'mp'), may hold values from -0.1875 to 0.1875
- w_out: bfloat16 [4096, 4096], P('mp'), may hold values from -0.09375 to 0.09375
- grad_out: bfloat16 [12288, 4096], P(('dp', 'mp')), may hold values from -6 to 6
Outputs:
- attended: bfloat16 [12288, 4096], P(('dp', 'mp'))
- grad_tokens: bfloat16 [12288, 4096], P(('dp', 'mp'))
- grad_encoded: float32 [128, 128, 1024], P('dp', None, 'mp')
Inputs may be any that keep to these rules, and one draw needn't show every extreme that they name: `neighbour_owner`: within one sequence's list no owner appears twice, and the list of sequence s names owner s.
All inputs are finite; a program needn't handle non-finite values.
Results may differ from a plain program's by a relative error of at most 0.017.
Values may be sent and summed in bfloat16 or wider, within the bound.
No kernel may reach another device: no remote copies, remote signals or barrier semaphores. Data moves between devices by JAX's collectives and lax.ppermute only.
A program may use at most 128 MiB of HBM per device.

v0:
```python
import functools
import math

import jax
import jax.numpy as jnp
from jax import lax
from jax.experimental import pallas as pl
from jax.experimental.pallas import tpu as pltpu
from jax.sharding import PartitionSpec as P

HD = 128
GROUP = 64
NBR = 2
XS = 4
CORES = 2
BF = jnp.bfloat16
F32 = jnp.float32
BIG = 56
B_PROJ = 56
B_ATT = 40
B_OUTS = 30
FIRST = 16
OUTS = 0.3
LAST = 65536
ATT = 1
NT = (((1,), (1,)), ((), ()))
TN = (((0,), (0,)), ((), ()))


def mm(a, b):
    return jnp.dot(a, b, preferred_element_type=F32)


def mm_nt(a, b):
    return lax.dot_general(a, b, NT, preferred_element_type=F32)


def mm_tn(a, b):
    return lax.dot_general(a, b, TN, preferred_element_type=F32)


def x_perm(step):
    return [(2 * x + c, 2 * ((x + step) % XS) + c) for x in range(XS) for c in range(CORES)]


CORE_SWAP = [(2 * x + c, 2 * x + 1 - c) for x in range(XS) for c in range(CORES)]


def x_pieces(block):
    return [block] + [lax.ppermute(block, "mp", x_perm(-i)) for i in range(1, XS)]


def swap(block):
    return lax.ppermute(block, "mp", CORE_SWAP)


def after(values, earlier):
    return lax.optimization_barrier((values, earlier))[0]


def by_distance(x, c):
    own = [2 * ((x + i) % XS) + c for i in range(XS)]
    other = [2 * ((x + i) % XS) + 1 - c for i in range(XS)]
    return jnp.stack(own + other).astype(jnp.int32)


ANY = pl.BlockSpec(memory_space=pl.ANY)
SMEM = pl.BlockSpec(memory_space=pltpu.SMEM)
VMEM = pl.BlockSpec(memory_space=pltpu.VMEM)


def params(mib):
    return pltpu.CompilerParams(vmem_limit_bytes=mib << 20)


def cost(flops, bytes_accessed):
    return pl.CostEstimate(flops=flops, bytes_accessed=bytes_accessed, transcendentals=0)


def project_kernel(*refs, cut, transposed):
    pieces = refs[:4]
    w_any, wx_any, out_ref, outx_ref, a_ref, w_ref, wx_ref, acc, accx, sems = refs[4:]
    rows = pieces[0].shape[0]
    steps = a_ref.shape[1] // cut
    copies = []
    for j, piece in enumerate(pieces):
        at = pl.ds(j * rows, rows)
        copies.append(pltpu.make_async_copy(piece, a_ref.at[at, :], sems.at[j]))
        copies[-1].start()

    def weights(k):
        part = pl.ds(pl.multiple_of(k * cut, cut), cut)
        at = (slice(None), part) if transposed else (part, slice(None))
        return [
            pltpu.make_async_copy(w_any.at[at], w_ref.at[at], sems.at[4 + 2 * k]),
            pltpu.make_async_copy(wx_any.at[at], wx_ref.at[at], sems.at[5 + 2 * k]),
        ]

    for k in range(steps):
        for copy in weights(k):
            copy.start()
    acc[...] = jnp.zeros(acc.shape, F32)
    accx[...] = jnp.zeros(accx.shape, F32)
    for copy in copies:
        copy.wait()

    def step(k, _):
        part = pl.ds(pl.multiple_of(k * cut, cut), cut)
        a = a_ref[:, part]
        for copy, w, total in zip(weights(k), (w_ref, wx_ref), (acc, accx)):
            copy.wait()
            total[...] += mm_nt(a, w[:, part]) if transposed else mm(a, w[part, :])
        return 0

    lax.fori_loop(0, steps, step, 0)
    out_ref[...] = acc[...].astype(BF)
    outx_ref[...] = accx[...].astype(BF)


def project(pieces, w, wx, transposed, name, weight=1):
    rows, depth = pieces[0].shape
    width = w.shape[0] if transposed else w.shape[1]
    length = rows * len(pieces)
    cut = depth // 8
    out = jax.ShapeDtypeStruct((length, width), BF)
    return pl.pallas_call(
        functools.partial(project_kernel, cut=cut, transposed=transposed),
        in_specs=[ANY] * 6,
        out_specs=[VMEM] * 2,
        scratch_shapes=[
            pltpu.VMEM((length, depth), BF),
            pltpu.VMEM(w.shape, BF),
            pltpu.VMEM(w.shape, BF),
            pltpu.VMEM((length, width), F32),
            pltpu.VMEM((length, width), F32),
            pltpu.SemaphoreType.DMA((4 + 2 * (depth // cut),)),
        ],
        out_shape=[out, out],
        compiler_params=params(B_PROJ),
        cost_estimate=cost(int(4 * length * depth * width * weight), 1 << 20),
        name=name,
    )(*pieces, w, wx)


def arrange_kernel(index_ref, wk_any, wv_any, wk_out, wv_out, sems):
    rows = wk_any.shape[0] // 8
    copies = []
    for j in range(8):
        at = pl.ds(pl.multiple_of(index_ref[j] * rows, rows), rows)
        put = pl.ds(j * rows, rows)
        for i, (w, o) in enumerate(((wk_any, wk_out), (wv_any, wv_out))):
            copies.append(pltpu.make_async_copy(w.at[at, :], o.at[put, :], sems.at[2 * j + i]))
            copies[-1].start()
    for copy in copies:
        copy.wait()


def arrange(indices, w_key, w_value):
    out = jax.ShapeDtypeStruct(w_key.shape, BF)
    return pl.pallas_call(
        arrange_kernel,
        in_specs=[SMEM, ANY, ANY],
        out_specs=[ANY] * 2,
        scratch_shapes=[pltpu.SemaphoreType.DMA((16,))],
        out_shape=[out, out],
        compiler_params=params(8),
        cost_estimate=cost(0, 1 << 20),
        name="arrange",
    )(indices, w_key, w_value)


def assemble_kernel(index_ref, *refs):
    parts, outs_ref = refs[:4], refs[4:]
    rows = outs_ref[0].shape[0] // 8
    for i in range(2):
        for j in range(8):
            at = pl.ds(pl.multiple_of(index_ref[j] * rows, 16), rows)
            part = slice(j % XS * rows, (j % XS + 1) * rows)
            outs_ref[i][at, :] = parts[2 * i + j // XS][part, :]


def assemble(indices, q, gh):
    out = jax.ShapeDtypeStruct((2 * q[0].shape[0], q[0].shape[1]), BF)
    return pl.pallas_call(
        assemble_kernel,
        in_specs=[SMEM] + [VMEM] * 4,
        out_specs=[VMEM] * 2,
        out_shape=[out, out],
        compiler_params=params(8),
        cost_estimate=cost(0, 1 << 20),
        name="assemble",
    )(indices, *q, *gh)


def attend_kernel(index_ref, *refs):
    pieces = refs[:8]
    q_any, gh_any, wk_any, wv_any, mine_any, theirs_any, keep_any, send_any = refs[8:16]
    near, q_ref, gh_ref, wk_ref, wv_ref, small, share, sems, out_sems = refs[16:]
    neigh, depth, _ = near.shape
    cols = pieces[0].shape[2]
    groups = neigh // NBR
    keys = NBR * depth
    heads = q_ref.shape[1] // HD
    scale = 1.0 / math.sqrt(HD)
    moves = [(wk_any, wk_ref)]
    for j in range(8):
        part = pl.ds(0, NBR)
        moves.append((pieces[j].at[part], near.at[part, :, pl.ds(j * cols, cols)]))
    moves += [(wv_any, wv_ref), (q_any, q_ref), (gh_any, gh_ref)]
    head = len(moves)
    later = pl.ds(NBR, neigh - NBR)
    for j in range(8):
        moves.append((pieces[j].at[later], near.at[later, :, pl.ds(j * cols, cols)]))
    copies = [pltpu.make_async_copy(s, d, sems.at[i]) for i, (s, d) in enumerate(moves)]
    for copy in copies:
        copy.start()
    part = [slice(h * HD, (h + 1) * HD) for h in range(heads)]

    def stores(g):
        two = pl.ds(g * NBR, NBR)
        return [
            pltpu.make_async_copy(share.at[pl.ds(0, XS), two], keep_any.at[:, two], out_sems.at[2 * g]),
            pltpu.make_async_copy(share.at[pl.ds(XS, XS), two], send_any.at[:, two], out_sems.at[2 * g + 1]),
        ]

    def group(g, _):
        own = pl.ds(pl.multiple_of(g * GROUP, GROUP), GROUP)
        two = pl.ds(g * NBR, NBR)

        @pl.when(g == 1)
        def _():
            for copy in copies[head:]:
                copy.wait()

        near_rows = near[two].reshape(keys, near.shape[2])
        k = mm(near_rows, wk_ref[...]).astype(BF)
        v = mm(near_rows, wv_ref[...]).astype(BF)
        q = q_ref[own, :]
        gh = gh_ref[own, :]
        s = jnp.concatenate([mm_nt(q[:, p], k[:, p]) for p in part], axis=0) * scale
        gp = jnp.concatenate([mm_nt(gh[:, p], v[:, p]) for p in part], axis=0)
        e = jnp.exp(s - jnp.max(s, axis=-1, keepdims=True))
        probs = e * (1.0 / jnp.sum(e, axis=-1, keepdims=True))
        pb = probs.astype(BF)
        centre = jnp.sum(probs * gp, axis=-1, keepdims=True)
        gs = (probs * (gp - centre) * scale).astype(BF)
        gk = []
        gv = []
        for h, p in enumerate(part):
            r = slice(h * GROUP, (h + 1) * GROUP)
            small[0, own, p] = mm(pb[r], v[:, p]).astype(BF)
            small[1, own, p] = mm(gs[r], k[:, p]).astype(BF)
            gk.append(mm_tn(gs[r], q[:, p]).astype(BF))
            gv.append(mm_tn(pb[r], gh[:, p]).astype(BF))
        gk = jnp.concatenate(gk, axis=1)
        gv = jnp.concatenate(gv, axis=1)
        for j in range(0, 8, 2):
            put = slice(j * cols, (j + 2) * cols)
            grad = (mm_nt(gk, wk_ref[put, :]) + mm_nt(gv, wv_ref[put, :])).astype(BF)
            share[j, two] = grad[:, :cols].reshape(NBR, depth, cols)
            share[j + 1, two] = grad[:, cols:].reshape(NBR, depth, cols)
        for copy in stores(g):
            copy.start()
        return 0

    for copy in copies[:head]:
        copy.wait()
    lax.fori_loop(0, groups, group, 0)
    rows = small.shape[1] // 8
    last = []
    for j in range(8):
        at = pl.ds(pl.multiple_of(index_ref[j] * rows, 16), rows)
        put = pl.ds(j % XS * rows, rows)
        dst = (mine_any, theirs_any)[j // XS].at[:, put, :]
        last.append(pltpu.make_async_copy(small.at[:, at, :], dst, out_sems.at[2 * groups + j]))
        last[-1].start()
    for g in range(groups):
        for copy in stores(g):
            copy.wait()
    for copy in last:
        copy.wait()


def attend(indices, pieces, q, gh, w_key, w_value):
    neigh, depth, cols = pieces[0].shape
    length, width = q.shape
    groups = neigh // NBR
    share = jax.ShapeDtypeStruct((XS, neigh, depth, cols), BF)
    half = jax.ShapeDtypeStruct((2, length // 2, width), BF)
    return pl.pallas_call(
        attend_kernel,
        in_specs=[SMEM] + [ANY] * 12,
        out_specs=[ANY] * 4,
        scratch_shapes=[
            pltpu.VMEM((neigh, depth, 8 * cols), BF),
            pltpu.VMEM((length, width), BF),
            pltpu.VMEM((length, width), BF),
            pltpu.VMEM(w_key.shape, BF),
            pltpu.VMEM(w_value.shape, BF),
            pltpu.VMEM((2, length, width), BF),
            pltpu.VMEM((8, neigh, depth, cols), BF),
            pltpu.SemaphoreType.DMA((20,)),
            pltpu.SemaphoreType.DMA((2 * groups + 8,)),
        ],
        out_shape=[half, half, share, share],
        compiler_params=params(B_ATT),
        cost_estimate=cost(int(ATT * 8 * neigh * depth * 8 * cols * width), 1 << 20),
        name="attend",
    )(indices, *pieces, q, gh, w_key, w_value)


def outs_kernel(mine_any, got_any, wq_any, wqx_any, wo_any, wox_any, *refs, cut):
    out_refs, (mine_ref, got_ref, wq_ref, wqx_ref, wo_ref, wox_ref, sems) = refs[:XS], refs[XS:]
    rows = mine_ref.shape[1] // XS
    steps = wq_ref.shape[0] // cut
    first = [
        pltpu.make_async_copy(mine_any, mine_ref, sems.at[4 * steps]),
        pltpu.make_async_copy(got_any, got_ref, sems.at[4 * steps + 1]),
    ]

    def weights(k):
        part = pl.ds(pl.multiple_of(k * cut, cut), cut)
        moves = [(w.at[part, :], r.at[part, :]) for w, r in ((wq_any, wq_ref), (wqx_any, wqx_ref))]
        moves += [(w.at[:, part], r.at[:, part]) for w, r in ((wo_any, wo_ref), (wox_any, wox_ref))]
        return [pltpu.make_async_copy(s, d, sems.at[4 * k + i]) for i, (s, d) in enumerate(moves)]

    for copy in first:
        copy.start()
    for k in range(steps):
        for copy in weights(k):
            copy.start()
    for copy in first:
        copy.wait()

    def step(k, _):
        for copy in weights(k):
            copy.wait()
        part = pl.ds(pl.multiple_of(k * cut, cut), cut)
        gt = mm_nt(mine_ref[1], wq_ref[part, :]) + mm_nt(got_ref[1], wqx_ref[part, :])
        at = mm(mine_ref[0], wo_ref[:, part]) + mm(got_ref[0], wox_ref[:, part])
        for i, r in enumerate((gt, at)):
            for j in range(XS):
                out_refs[j][i, :, part] = r[j * rows : (j + 1) * rows].astype(BF)
        return 0

    lax.fori_loop(0, steps, step, 0)


def outs(mine, got, w_query, wx_query, w_out, wx_out):
    _, length, width = mine.shape
    full = w_query.shape[0]
    cut = full // 8
    return pl.pallas_call(
        functools.partial(outs_kernel, cut=cut),
        in_specs=[ANY] * 6,
        out_specs=[VMEM] * XS,
        scratch_shapes=[
            pltpu.VMEM(mine.shape, BF),
            pltpu.VMEM(mine.shape, BF),
            pltpu.VMEM(w_query.shape, BF),
            pltpu.VMEM(w_query.shape, BF),
            pltpu.VMEM(w_out.shape, BF),
            pltpu.VMEM(w_out.shape, BF),
            pltpu.SemaphoreType.DMA((4 * (full // cut) + 2,)),
        ],
        out_shape=[jax.ShapeDtypeStruct((2, length // XS, full), BF)] * XS,
        compiler_params=params(B_OUTS),
        cost_estimate=cost(int(OUTS * 8 * length * width * full), int(OUTS * (16 << 20))),
        name="outs",
    )(mine, got, w_query, wx_query, w_out, wx_out)


def pick_kernel(index_ref, table_ref, *out_refs):
    at = 0
    for out in out_refs:
        for i in range(out.shape[0]):
            out[i] = table_ref[index_ref[at]]
            at += 1


def pick(index, table, counts, name):
    rest = table.shape[1:]
    return pl.pallas_call(
        pick_kernel,
        in_specs=[SMEM, VMEM],
        out_specs=[VMEM] * len(counts),
        out_shape=[jax.ShapeDtypeStruct((n, *rest), table.dtype) for n in counts],
        compiler_params=params(16),
        cost_estimate=cost(0, 1 << 20),
        name=name,
    )(index, table)


def outgoing_kernel(slot_ref, at_ref, table_any, out_ref, part, sem):
    cols = out_ref.shape[2]
    at = pl.ds(pl.multiple_of(at_ref[0] * cols, cols), cols)
    copy = pltpu.make_async_copy(table_any.at[:, :, at], part, sem)
    copy.start()
    copy.wait()
    for i in range(out_ref.shape[0]):
        out_ref[i] = part[slot_ref[i]]


def choose_outgoing(slot, at, table, cols):
    count, depth, _ = table.shape
    return pl.pallas_call(
        outgoing_kernel,
        in_specs=[SMEM, SMEM, ANY],
        out_specs=VMEM,
        scratch_shapes=[pltpu.VMEM((count, depth, cols), BF), pltpu.SemaphoreType.DMA(())],
        out_shape=jax.ShapeDtypeStruct((slot.shape[0], depth, cols), BF),
        compiler_params=params(BIG),
        cost_estimate=cost(0, 1 << 20),
        name="outgoing",
    )(slot, at, table)


def place_kernel(place_ref, *refs):
    out_ref, total = refs[-2:]
    at = 0
    for i in range(0, len(refs) - 2, XS):
        n = refs[i].shape[0]
        acc = refs[i][...].astype(F32)
        for r in refs[i + 1 : i + XS]:
            acc = acc + r[...].astype(F32)
        total[at : at + n] = acc.astype(BF)
        at += n
    for i in range(out_ref.shape[0]):
        out_ref[i] = total[place_ref[i]]


def place_sums(place, parts):
    flat = [p for chunk in parts for p in chunk]
    rest = flat[0].shape[1:]
    neigh = sum(chunk[0].shape[0] for chunk in parts)
    return pl.pallas_call(
        place_kernel,
        grid_spec=pltpu.PrefetchScalarGridSpec(
            num_scalar_prefetch=1,
            grid=(1,),
            in_specs=[pl.BlockSpec(p.shape, lambda i, s: (0, 0, 0)) for p in flat],
            out_specs=pl.BlockSpec((place.shape[0], *rest), lambda i, s: (0, 0, 0)),
            scratch_shapes=[pltpu.VMEM((neigh, *rest), BF)],
        ),
        out_shape=jax.ShapeDtypeStruct((place.shape[0], *rest), BF),
        compiler_params=params(16),
        cost_estimate=cost(0, 4 << 20),
        name="place",
    )(place, *flat)


def collect_kernel(slot_ref, held_ref, in_ref, out_ref):
    out_ref[...] = jnp.zeros(out_ref.shape, F32)
    for i in range(in_ref.shape[0]):

        @pl.when(held_ref[i] > 0)
        def _():
            out_ref[slot_ref[i]] += in_ref[i].astype(F32)


def collect(slot, held, returned, count):
    rest = returned.shape[1:]
    return pl.pallas_call(
        collect_kernel,
        in_specs=[SMEM, SMEM, VMEM],
        out_specs=VMEM,
        out_shape=jax.ShapeDtypeStruct((count, *rest), F32),
        compiler_params=params(16),
        cost_estimate=cost(0, 2 << 20),
        name="collect",
    )(slot, held, returned)


def final_kernel(*refs):
    total = refs[0][...].astype(F32)
    for r in refs[1:XS]:
        total = total + r[...].astype(F32)
    total = total.astype(BF)
    refs[XS][...] = total[0]
    refs[XS + 1][...] = total[1]


def final_sums(parts):
    two, rows, full = parts[0].shape
    cut = 1024
    out = jax.ShapeDtypeStruct((rows, full), BF)
    return pl.pallas_call(
        final_kernel,
        grid=(full // cut,),
        in_specs=[pl.BlockSpec((two, rows, cut), lambda i: (0, 0, i))] * XS,
        out_specs=[pl.BlockSpec((rows, cut), lambda i: (0, i))] * 2,
        out_shape=[out, out],
        compiler_params=params(16),
        cost_estimate=cost(LAST << 20, 4 << 20),
        name="final",
    )(*parts)


def chip_sums(keep, got):
    return [(keep[i].astype(F32) + got[i].astype(F32)).astype(BF) for i in range(XS)]


def x_parts(sums):
    return sums[:1] + [lax.ppermute(sums[i], "mp", x_perm(i)) for i in range(1, XS)]


def body(
    tokens, encoded, neighbour_owner, neighbour_slot, w_query, w_key, w_value, w_out, grad_out
):
    dp_count = lax.axis_size("dp")
    dp_at = lax.axis_index("dp")
    mp_at = lax.axis_index("mp")
    x, c = mp_at // CORES, mp_at % CORES
    neigh = neighbour_owner.shape[1] * NBR
    share = encoded.shape[2] // (XS * CORES)
    indices = by_distance(x, c)

    owners_all = neighbour_owner.reshape(dp_count, neigh)
    slots_all = neighbour_slot.reshape(dp_count, neigh)
    held_here = owners_all == dp_at
    held = jnp.any(held_here, axis=1).astype(jnp.int32)
    held_slot = jnp.sum(jnp.where(held_here, slots_all, 0), axis=1).astype(jnp.int32)
    my_owners = lax.dynamic_index_in_dim(owners_all, dp_at, 0, keepdims=False)
    place = jnp.argmax(my_owners[None, :] == jnp.arange(dp_count)[:, None], axis=1).astype(
        jnp.int32
    )

    t_own = x_pieces(tokens)
    g_own = x_pieces(grad_out)
    outgoing = choose_outgoing(held_slot, mp_at[None].astype(jnp.int32), encoded, share)
    arrived = lax.all_to_all(outgoing, "dp", split_axis=0, concat_axis=0, tiled=True)
    wx_query, wx_out = swap(w_query), swap(w_out)
    q_own, q_send = project(
        t_own, w_query, wx_query, False, "query", FIRST
    )
    q_got = swap(q_send)
    w_key, w_value = arrange(indices, after(w_key, q_own), w_value)
    (near,) = pick(my_owners, after(arrived, (q_own, q_got, g_own, w_key)), [neigh], "nearby")
    gh_own, gh_send = project(after(g_own, near), w_out, wx_out, True, "gheads", 0)
    near = x_pieces(near)
    gh_got = swap(gh_send)
    query, grad_heads = assemble(indices, (q_own, q_got), (gh_own, gh_got))
    own = [after(piece, grad_heads) for piece in near]
    pieces = own + [swap(piece) for piece in own]
    mine, theirs, keep, send = attend(indices, pieces, query, grad_heads, w_key, w_value)
    sums = chip_sums(keep, swap(send))
    parts = [x_parts(sums)]
    sums2 = list(
        outs(after(mine, sums), swap(theirs), w_query, wx_query, w_out, wx_out)
    )
    parts2 = x_parts(after(sums2, parts))
    parts = after(parts, sums2)
    returned = lax.all_to_all(
        place_sums(place, parts), "dp", split_axis=0, concat_axis=0, tiled=True
    )
    grad_tokens, attended = final_sums(parts2)
    grad_encoded = collect(held_slot, held, after(returned, attended), encoded.shape[0])
    return (attended, grad_tokens, grad_encoded)


def solution(mesh):
    placed = (
        P(("dp", "mp"), None),
        P("dp", None, None),
        P(),
        P(),
        P(None, "mp"),
        P(None, "mp"),
        P(None, "mp"),
        P("mp", None),
        P(("dp", "mp"), None),
    )
    return jax.shard_map(
        body,
        mesh=mesh,
        in_specs=placed,
        out_specs=(P(("dp", "mp"), None), P(("dp", "mp"), None), P("dp", None, "mp")),
        check_vma=False,
    )
```

profile of v0, /device:TPU:8, one launch (start us, length us, event | category | flops | bytes accessed | tf_op | source)
XLA Modules:
  0.0 158.9 jit_solution(5244414899475915936)
XLA Ops:
  0.6 0.1 collective-permute-start.3
  0.7 0.5 collective-permute-start.8
  1.2 3.0 %collective-permute-start.1 = (bf16[48,4096]{1,0:T(8,128)(2,1)}, bf16[48,4096]{1,0:T(8,128)(2,1)}, u32[]{:S(2)}, u32[]{:S(2)}) collective-permute-start(bf16[48,4096]{1,0:T(8,128)(2,1)} %refs_0_.1), channel_id=1, source_target_pairs={{0,4},{1,5},{2,6},{3,7},{4,0},{5,1},{6,2},{7,3},{8,12},{9,13},{10,... | collective-permute-start | bytes 1179656 | tf_op jit(solution)/shard_map/ppermute | solution.py:50
  4.3 1.1 collective-permute-start
  5.4 0.9 collective-permute-start.2
  6.3 1.3 select_reduce_fusion.slot_ref
  7.5 2.7 %outgoing.1 = bf16[32,128,128]{2,1,0:T(8,128)(2,1)} custom-call(s32[32]{0:T(128)} %select_reduce_fusion.slot_ref, s32[1]{0:T(128)} %bitcast.9.at_ref, bf16[4,128,1024]{2,1,0:T(8,128)(2,1)} %table_any.1), custom_call_target="tpu_custom_call" | custom-call | bytes 1048576 | tf_op jit(solution)/shard_map/outgoing/pallas_call | solution.py:406
  10.2 11.7 %all-to-all-start = ((bf16[32,128,128]{2,1,0:T(8,128)(2,1)}), bf16[32,128,128]{2,1,0:T(8,128)(2,1)S(1)}, u32[]{:S(2)}, u32[]{:S(2)}) async-start(bf16[32,128,128]{2,1,0:T(8,128)(2,1)} %outgoing.1), calls=%async_computation | async-start | bytes 2097152 | tf_op jit(solution)/shard_map/all_to_all | solution.py:531
  21.9 0.0 copy-start.11
  22.0 0.0 copy-start.2
  22.0 0.0 copy-start.3
  22.0 0.0 collective-permute-done.1.refs_2_
  22.0 0.7 collective-permute-start.7
  22.7 0.1 collective-permute-done.refs_1_
  22.7 3.2 %collective-permute-start.6 = (bf16[48,4096]{1,0:T(8,128)(2,1)}, bf16[48,4096]{1,0:T(8,128)(2,1)}, u32[]{:S(2)}, u32[]{:S(2)}) collective-permute-start(bf16[48,4096]{1,0:T(8,128)(2,1)} %refs_0_.2), channel_id=1, source_target_pairs={{0,4},{1,5},{2,6},{3,7},{4,0},{5,1},{6,2},{7,3},{8,12},{9,13},{10,... | collective-permute-start | bytes 1179656 | tf_op jit(solution)/shard_map/ppermute | solution.py:50
  25.9 0.9 collective-permute-start.5
  26.8 6.8 %query.1 = (bf16[192,512]{1,0:T(8,128)(2,1)}, bf16[192,512]{1,0:T(8,128)(2,1)}) custom-call(bf16[48,4096]{1,0:T(8,128)(2,1)} %refs_0_.1, bf16[48,4096]{1,0:T(8,128)(2,1)} %collective-permute-done.refs_1_, bf16[48,4096]{1,0:T(8,128)(2,1)} %collective-permute-done.1.refs_2_, bf16[48,4096]{1,0:T(8,128)(2,1)} %collective-permute-done.2.refs_3_, ...), custom_call_target="tpu_custom_call" | custom-call | flops 25769803776 | bytes 1048576 | tf_op jit(solution)/shard_map/query/pallas_call | solution.py:126
  33.6 0.1 collective-permute-start.4
  33.8 0.1 constant_dynamic-slice_fusion
  33.9 0.1 copy.14
  34.0 0.1 stack.35.index_ref
  34.1 3.4 %arrange.1 = (bf16[1024,512]{1,0:T(8,128)(2,1)S(1)}, bf16[1024,512]{1,0:T(8,128)(2,1)S(1)}) custom-call(s32[8]{0:T(128)S(1)} %stack.35.index_ref, bf16[1024,512]{1,0:T(8,128)(2,1)S(1)} %copy-done.2, bf16[1024,512]{1,0:T(8,128)(2,1)S(1)} %copy-done.3), custom_call_target="tpu_custom_call" | custom-call | bytes 1048576 | tf_op jit(solution)/shard_map/arrange/pallas_call | solution.py:160
  37.6 1.0 copy-done.7
  38.6 1.0 copy-done.9
  39.6 2.8 %collective-permute-done.6.refs_2_ = bf16[48,4096]{1,0:T(8,128)(2,1)} collective-permute-done((bf16[48,4096]{1,0:T(8,128)(2,1)}, bf16[48,4096]{1,0:T(8,128)(2,1)}, u32[]{:S(2)}, u32[]{:S(2)}) %collective-permute-start.6) | collective-permute-done | bytes 393248 | tf_op jit(solution)/shard_map/ppermute | solution.py:50
  42.3 1.7 %collective-permute-done.5.refs_1_ = bf16[48,4096]{1,0:T(8,128)(2,1)} collective-permute-done((bf16[48,4096]{1,0:T(8,128)(2,1)}, bf16[48,4096]{1,0:T(8,128)(2,1)}, u32[]{:S(2)}, u32[]{:S(2)}) %collective-permute-start.5) | collective-permute-done | bytes 393248 | tf_op jit(solution)/shard_map/ppermute | solution.py:50
  44.0 5.4 %all-to-all-done.table_ref = bf16[32,128,128]{2,1,0:T(8,128)(2,1)S(1)} async-done(((bf16[32,128,128]{2,1,0:T(8,128)(2,1)}), bf16[32,128,128]{2,1,0:T(8,128)(2,1)S(1)}, u32[]{:S(2)}, u32[]{:S(2)}) %all-to-all-start) | async-done | bytes 1048608 | tf_op jit(solution)/shard_map/all_to_all | solution.py:531
  49.4 0.6 nearby.1.refs_0_
  50.0 0.0 copy-start.4
  50.0 0.7 collective-permute-start.12
  50.7 3.2 %collective-permute-start.11 = (bf16[12,128,128]{2,1,0:T(8,128)(2,1)S(1)}, bf16[12,128,128]{2,1,0:T(8,128)(2,1)S(1)}, u32[]{:S(2)}, u32[]{:S(2)}) collective-permute-start(bf16[12,128,128]{2,1,0:T(8,128)(2,1)S(1)} %nearby.1.refs_0_), channel_id=1, source_target_pairs={{0,4},{1,5},{2,6},{3,7},{4,0},{5,1},{6,2},{7,3},{8,12},{9,13},{10,... | collective-permute-start | bytes 1179656 | tf_op jit(solution)/shard_map/ppermute | solution.py:50
  53.9 7.9 %gheads.1 = (bf16[192,512]{1,0:T(8,128)(2,1)}, bf16[192,512]{1,0:T(8,128)(2,1)}) custom-call(bf16[48,4096]{1,0:T(8,128)(2,1)} %refs_0_.2, bf16[48,4096]{1,0:T(8,128)(2,1)} %collective-permute-done.5.refs_1_, bf16[48,4096]{1,0:T(8,128)(2,1)} %collective-permute-done.6.refs_2_, bf16[48,4096]{1,0:T(8,128)(2,1)} %collective-permute-done.7.refs_3_, ...), custom_call_target="tpu_custom_call" | custom-call | bytes 1048576 | tf_op jit(solution)/shard_map/gheads/pallas_call | solution.py:126
  61.8 0.1 collective-permute-start.9
  61.9 1.6 %collective-permute-done.9.refs_3_ = bf16[192,512]{1,0:T(8,128)(2,1)S(1)} collective-permute-done((bf16[192,512]{1,0:T(8,128)(2,1)}, bf16[192,512]{1,0:T(8,128)(2,1)S(1)}, u32[]{:S(2)}, u32[]{:S(2)}) %collective-permute-start.9) | collective-permute-done | bytes 196640 | tf_op jit(solution)/shard_map/ppermute | solution.py:54
  63.6 0.9 copy-done.5
  64.5 0.6 assemble.1
  65.1 0.2 collective-permute-start.13
  65.3 3.5 %collective-permute-done.11.refs_2_ = bf16[12,128,128]{2,1,0:T(8,128)(2,1)S(1)} collective-permute-done((bf16[12,128,128]{2,1,0:T(8,128)(2,1)S(1)}, bf16[12,128,128]{2,1,0:T(8,128)(2,1)S(1)}, u32[]{:S(2)}, u32[]{:S(2)}) %collective-permute-start.11) | collective-permute-done | bytes 393248 | tf_op jit(solution)/shard_map/ppermute | solution.py:50
  68.9 0.0 collective-permute-done.10.refs_1_
  68.9 0.5 collective-permute-start.15
  69.4 0.0 collective-permute-start.16
  69.4 1.2 collective-permute-done.14.refs_5_
  70.6 0.6 collective-permute-done.15.refs_6_
  71.2 0.6 collective-permute-done.16.refs_7_
  71.8 15.7 %attend.1 = (bf16[2,192,512]{2,1,0:T(8,128)(2,1)S(1)}, bf16[2,192,512]{2,1,0:T(8,128)(2,1)S(1)}, bf16[4,12,128,128]{3,2,1,0:T(8,128)(2,1)S(1)}, bf16[4,12,128,128]{3,2,1,0:T(8,128)(2,1)S(1)}) custom-call(s32[8]{0:T(128)S(1)} %stack.35.index_ref, bf16[12,128,128]{2,1,0:T(8,128)(2,1)S(1)} %nearby.1.refs_0_, ...), custom_call_target="tpu_custom_call" | custom-call | flops 6442450944 | bytes 1048576 | tf_op jit(solution)/shard_map/attend/pallas_call | solution.py:290
  87.5 0.2 collective-permute-start.17
  87.7 0.4 collective-permute-start.18
  88.1 2.9 %collective-permute-done.17 = bf16[4,12,128,128]{3,2,1,0:T(8,128)(2,1)S(1)} collective-permute-done((bf16[4,12,128,128]{3,2,1,0:T(8,128)(2,1)S(1)}, bf16[4,12,128,128]{3,2,1,0:T(8,128)(2,1)S(1)}, u32[]{:S(2)}, u32[]{:S(2)}) %collective-permute-start.17) | collective-permute-done | bytes 1572896 | tf_op jit(solution)/shard_map/ppermute | solution.py:54
  91.0 0.8 fusion.3
  91.7 2.7 %collective-permute-start.21 = (bf16[12,128,128]{2,1,0:T(8,128)(2,1)S(1)}, bf16[12,128,128]{2,1,0:T(8,128)(2,1)S(1)}, u32[]{:S(2)}, u32[]{:S(2)}) collective-permute-start(bf16[12,128,128]{2,1,0:T(8,128)(2,1)S(1)} %get-tuple-element.81), channel_id=1, source_target_pairs={{0,6},{1,7},{2,0},{3,1},{4,2},{5,3},{6,4},{7,5},{8,14},{9,15},{10,... | collective-permute-start | bytes 1179656 | tf_op jit(solution)/shard_map/ppermute | solution.py:504
  94.4 1.0 collective-permute-start.19
  95.4 8.8 %outs.1 = (bf16[2,48,4096]{2,1,0:T(8,128)(2,1)S(1)}, bf16[2,48,4096]{2,1,0:T(8,128)(2,1)}, bf16[2,48,4096]{2,1,0:T(8,128)(2,1)}, bf16[2,48,4096]{2,1,0:T(8,128)(2,1)S(1)}) custom-call(bf16[2,192,512]{2,1,0:T(8,128)(2,1)S(1)} %get-tuple-element.63.mine_any, bf16[2,192,512]{2,1,0:T(8,128)(2,1)S(1)} %collective-permute-done.18.got_any, ...), custom_call_target="tpu_custom_call" | custom-call | flops 966367616 | bytes 5033164 | tf_op jit(solution)/shard_map/outs/pallas_call | solution.py:353
  104.2 7.4 %collective-permute-done.21.refs_3_ = bf16[12,128,128]{2,1,0:T(8,128)(2,1)S(1)} collective-permute-done((bf16[12,128,128]{2,1,0:T(8,128)(2,1)S(1)}, bf16[12,128,128]{2,1,0:T(8,128)(2,1)S(1)}, u32[]{:S(2)}, u32[]{:S(2)}) %collective-permute-start.21) | collective-permute-done | bytes 393248 | tf_op jit(solution)/shard_map/ppermute | solution.py:504
  111.6 3.4 %collective-permute-done.19.refs_1_ = bf16[12,128,128]{2,1,0:T(8,128)(2,1)S(1)} collective-permute-done((bf16[12,128,128]{2,1,0:T(8,128)(2,1)S(1)}, bf16[12,128,128]{2,1,0:T(8,128)(2,1)S(1)}, u32[]{:S(2)}, u32[]{:S(2)}) %collective-permute-start.19) | collective-permute-done | bytes 393248 | tf_op jit(solution)/shard_map/ppermute | solution.py:504
  115.0 2.4 %collective-permute-start.23 = (bf16[2,48,4096]{2,1,0:T(8,128)(2,1)}, bf16[2,48,4096]{2,1,0:T(8,128)(2,1)}, u32[]{:S(2)}, u32[]{:S(2)}) collective-permute-start(bf16[2,48,4096]{2,1,0:T(8,128)(2,1)} %get-tuple-element.71), channel_id=1, source_target_pairs={{0,4},{1,5},{2,6},{3,7},{4,0},{5,1},{6,2},{7,3},{8,12},{9,13},{10,... | collective-permute-start | bytes 2359304 | tf_op jit(solution)/shard_map/ppermute | solution.py:504
  117.3 0.9 collective-permute-start.24
  118.2 0.6 iota_reduce_fusion
  118.8 1.9 %place.1 = bf16[32,128,128]{2,1,0:T(8,128)(2,1)} custom-call(s32[32]{0:T(128)S(1)} %get-tuple-element.75.place_ref, bf16[12,128,128]{2,1,0:T(8,128)(2,1)S(1)} %get-tuple-element.76.refs_0_, bf16[12,128,128]{2,1,0:T(8,128)(2,1)S(1)} %collective-permute-done.19.refs_1_, bf16[12,128,128]{2,1,0:T(8,128)(2,1)S(1)} %collective-permute-done.20.refs_2_, ...), custom_call_target="tpu_custom_call" | custom-call | bytes 4194304 | tf_op jit(solution)/shard_map/place/pallas_call | solution.py:436
  120.8 9.0 %all-to-all-start.1 = ((bf16[32,128,128]{2,1,0:T(8,128)(2,1)}), bf16[32,128,128]{2,1,0:T(8,128)(2,1)S(1)}, u32[]{:S(2)}, u32[]{:S(2)}) async-start(bf16[32,128,128]{2,1,0:T(8,128)(2,1)} %place.1), calls=%async_computation.1 | async-start | bytes 2097152 | tf_op jit(solution)/shard_map/all_to_all | solution.py:553
  129.8 22.7 %collective-permute-done.22.refs_1_ = bf16[2,48,4096]{2,1,0:T(8,128)(2,1)} collective-permute-done((bf16[2,48,4096]{2,1,0:T(8,128)(2,1)}, bf16[2,48,4096]{2,1,0:T(8,128)(2,1)}, u32[]{:S(2)}, u32[]{:S(2)}) %collective-permute-start.22) | collective-permute-done | bytes 786464 | tf_op jit(solution)/shard_map/ppermute | solution.py:504
  152.5 0.6 collective-permute-done.24.refs_3_
  153.1 3.7 %final.1 = (bf16[48,4096]{1,0:T(8,128)(2,1)}, bf16[48,4096]{1,0:T(8,128)(2,1)}) custom-call(bf16[2,48,4096]{2,1,0:T(8,128)(2,1)S(1)} %get-tuple-element.69.refs_0_, bf16[2,48,4096]{2,1,0:T(8,128)(2,1)} %collective-permute-done.22.refs_1_, bf16[2,48,4096]{2,1,0:T(8,128)(2,1)} %collective-permute-done.23.refs_2_, ...), custom_call_target="tpu_custom_call" | custom-call | flops 68719476736 | bytes 4194304 | tf_op jit(solution)/shard_map/final/pallas_call | solution.py:487
  156.8 0.5 all-to-all-done.1.in_ref
  157.3 1.5 collect.1
  (34 shorter events, 0.1 us)
Async XLA Ops:
  0.6 26.1 %collective-permute-start.3 = (bf16[4096,512]{1,0:T(8,128)(2,1)}, bf16[4096,512]{1,0:T(8,128)(2,1)}, u32[]{:S(2)}, u32[]{:S(2)}) collective-permute-start(bf16[4096,512]{1,0:T(8,128)(2,1)} %wq_any.1), channel_id=1, source_target_pairs={{0,1},{1,0},{2,3},{3,2},{4,5},{5,4},{6,7},{7,6},{8,9},{9,8},{10,11... | collective-permute-start | bytes 12582920 | tf_op jit(solution)/shard_map/ppermute | solution.py:54
  0.7 53.2 %collective-permute-start.8 = (bf16[512,4096]{1,0:T(8,128)(2,1)}, bf16[512,4096]{1,0:T(8,128)(2,1)}, u32[]{:S(2)}, u32[]{:S(2)}) collective-permute-start(bf16[512,4096]{1,0:T(8,128)(2,1)} %wo_any.1), channel_id=1, source_target_pairs={{0,1},{1,0},{2,3},{3,2},{4,5},{5,4},{6,7},{7,6},{8,9},{9,8},{10,11... | collective-permute-start | bytes 12582920 | tf_op jit(solution)/shard_map/ppermute | solution.py:54
  1.2 20.8 %collective-permute-start.1 = (bf16[48,4096]{1,0:T(8,128)(2,1)}, bf16[48,4096]{1,0:T(8,128)(2,1)}, u32[]{:S(2)}, u32[]{:S(2)}) collective-permute-start(bf16[48,4096]{1,0:T(8,128)(2,1)} %refs_0_.1), channel_id=1, source_target_pairs={{0,4},{1,5},{2,6},{3,7},{4,0},{5,1},{6,2},{7,3},{8,12},{9,13},{10,... | collective-permute-start | bytes 1179656 | tf_op jit(solution)/shard_map/ppermute | solution.py:50
  4.3 18.5 %collective-permute-start = (bf16[48,4096]{1,0:T(8,128)(2,1)}, bf16[48,4096]{1,0:T(8,128)(2,1)}, u32[]{:S(2)}, u32[]{:S(2)}) collective-permute-start(bf16[48,4096]{1,0:T(8,128)(2,1)} %refs_0_.1), channel_id=1, source_target_pairs={{0,6},{1,7},{2,0},{3,1},{4,2},{5,3},{6,4},{7,5},{8,14},{9,15},{10,... | collective-permute-start | bytes 1179656 | tf_op jit(solution)/shard_map/ppermute | solution.py:50
  5.4 20.5 %collective-permute-start.2 = (bf16[48,4096]{1,0:T(8,128)(2,1)}, bf16[48,4096]{1,0:T(8,128)(2,1)}, u32[]{:S(2)}, u32[]{:S(2)}) collective-permute-start(bf16[48,4096]{1,0:T(8,128)(2,1)} %refs_0_.1), channel_id=1, source_target_pairs={{0,2},{1,3},{2,4},{3,5},{4,6},{5,7},{6,0},{7,1},{8,10},{9,11},{10,... | collective-permute-start | bytes 1179656 | tf_op jit(solution)/shard_map/ppermute | solution.py:50
  10.2 39.2 %all-to-all-start = ((bf16[32,128,128]{2,1,0:T(8,128)(2,1)}), bf16[32,128,128]{2,1,0:T(8,128)(2,1)S(1)}, u32[]{:S(2)}, u32[]{:S(2)}) async-start(bf16[32,128,128]{2,1,0:T(8,128)(2,1)} %outgoing.1), calls=%async_computation | async-start | bytes 2097152 | tf_op jit(solution)/shard_map/all_to_all | solution.py:531
  21.9 11.9 %copy-start.11 = (s32[32,6,2]{0,2,1:T(2,128)S(1)}, s32[32,6,2]{0,2,1:T(2,128)}, u32[]{:S(2)}) copy-start(s32[32,6,2]{0,2,1:T(2,128)} %param.11) | copy-start | bytes 4612
  22.0 12.1 %copy-start.2 = (bf16[1024,512]{1,0:T(8,128)(2,1)S(1)}, bf16[1024,512]{1,0:T(8,128)(2,1)}, u32[]{:S(2)}) copy-start(bf16[1024,512]{1,0:T(8,128)(2,1)} %wk_any) | copy-start | bytes 3145732
  22.0 12.1 %copy-start.3 = (bf16[1024,512]{1,0:T(8,128)(2,1)S(1)}, bf16[1024,512]{1,0:T(8,128)(2,1)}, u32[]{:S(2)}) copy-start(bf16[1024,512]{1,0:T(8,128)(2,1)} %wv_any.1) | copy-start | bytes 3145732
  22.0 17.6 %collective-permute-start.7 = (bf16[48,4096]{1,0:T(8,128)(2,1)}, bf16[48,4096]{1,0:T(8,128)(2,1)}, u32[]{:S(2)}, u32[]{:S(2)}) collective-permute-start(bf16[48,4096]{1,0:T(8,128)(2,1)} %refs_0_.2), channel_id=1, source_target_pairs={{0,2},{1,3},{2,4},{3,5},{4,6},{5,7},{6,0},{7,1},{8,10},{9,11},{10,... | collective-permute-start | bytes 1179656 | tf_op jit(solution)/shard_map/ppermute | solution.py:50
  22.7 19.6 %collective-permute-start.6 = (bf16[48,4096]{1,0:T(8,128)(2,1)}, bf16[48,4096]{1,0:T(8,128)(2,1)}, u32[]{:S(2)}, u32[]{:S(2)}) collective-permute-start(bf16[48,4096]{1,0:T(8,128)(2,1)} %refs_0_.2), channel_id=1, source_target_pairs={{0,4},{1,5},{2,6},{3,7},{4,0},{5,1},{6,2},{7,3},{8,12},{9,13},{10,... | collective-permute-start | bytes 1179656 | tf_op jit(solution)/shard_map/ppermute | solution.py:50
  25.9 18.1 %collective-permute-start.5 = (bf16[48,4096]{1,0:T(8,128)(2,1)}, bf16[48,4096]{1,0:T(8,128)(2,1)}, u32[]{:S(2)}, u32[]{:S(2)}) collective-permute-start(bf16[48,4096]{1,0:T(8,128)(2,1)} %refs_0_.2), channel_id=1, source_target_pairs={{0,6},{1,7},{2,0},{3,1},{4,2},{5,3},{6,4},{7,5},{8,14},{9,15},{10,... | collective-permute-start | bytes 1179656 | tf_op jit(solution)/shard_map/ppermute | solution.py:50
  33.6 15.8 %collective-permute-start.4 = (bf16[192,512]{1,0:T(8,128)(2,1)}, bf16[192,512]{1,0:T(8,128)(2,1)S(1)}, u32[]{:S(2)}, u32[]{:S(2)}) collective-permute-start(bf16[192,512]{1,0:T(8,128)(2,1)} %get-tuple-element.43), channel_id=1, source_target_pairs={{0,1},{1,0},{2,3},{3,2},{4,5},{5,4},{6,7},{7,6},{8,9},{9,8},{10,11... | collective-permute-start | bytes 589832 | tf_op jit(solution)/shard_map/ppermute | solution.py:54
  37.6 1.0 copy-start.7
  38.6 1.0 copy-start.9
  50.0 13.6 %copy-start.4 = (bf16[192,512]{1,0:T(8,128)(2,1)S(1)}, bf16[192,512]{1,0:T(8,128)(2,1)}, u32[]{:S(2)}) copy-start(bf16[192,512]{1,0:T(8,128)(2,1)} %get-tuple-element.42.refs_0_) | copy-start | bytes 589828
  50.0 21.7 %copy-start.8 = (bf16[1024,512]{1,0:T(8,128)(2,1)S(1)}, bf16[1024,512]{1,0:T(8,128)(2,1)}, u32[]{:S(2)}) copy-start(bf16[1024,512]{1,0:T(8,128)(2,1)} %copy-done.7) | copy-start | bytes 3145732
  50.0 21.7 %copy-start.10 = (bf16[1024,512]{1,0:T(8,128)(2,1)S(1)}, bf16[1024,512]{1,0:T(8,128)(2,1)}, u32[]{:S(2)}) copy-start(bf16[1024,512]{1,0:T(8,128)(2,1)} %copy-done.9) | copy-start | bytes 3145732
  50.0 15.3 %collective-permute-start.12 = (bf16[12,128,128]{2,1,0:T(8,128)(2,1)S(1)}, bf16[12,128,128]{2,1,0:T(8,128)(2,1)S(1)}, u32[]{:S(2)}, u32[]{:S(2)}) collective-permute-start(bf16[12,128,128]{2,1,0:T(8,128)(2,1)S(1)} %nearby.1.refs_0_), channel_id=1, source_target_pairs={{0,2},{1,3},{2,4},{3,5},{4,6},{5,7},{6,0},{7,1},{8,10},{9,11},{10,... | collective-permute-start | bytes 1179656 | tf_op jit(solution)/shard_map/ppermute | solution.py:50
  50.7 18.1 %collective-permute-start.11 = (bf16[12,128,128]{2,1,0:T(8,128)(2,1)S(1)}, bf16[12,128,128]{2,1,0:T(8,128)(2,1)S(1)}, u32[]{:S(2)}, u32[]{:S(2)}) collective-permute-start(bf16[12,128,128]{2,1,0:T(8,128)(2,1)S(1)} %nearby.1.refs_0_), channel_id=1, source_target_pairs={{0,4},{1,5},{2,6},{3,7},{4,0},{5,1},{6,2},{7,3},{8,12},{9,13},{10,... | collective-permute-start | bytes 1179656 | tf_op jit(solution)/shard_map/ppermute | solution.py:50
  53.9 15.0 %collective-permute-start.10 = (bf16[12,128,128]{2,1,0:T(8,128)(2,1)S(1)}, bf16[12,128,128]{2,1,0:T(8,128)(2,1)S(1)}, u32[]{:S(2)}, u32[]{:S(2)}) collective-permute-start(bf16[12,128,128]{2,1,0:T(8,128)(2,1)S(1)} %nearby.1.refs_0_), channel_id=1, source_target_pairs={{0,6},{1,7},{2,0},{3,1},{4,2},{5,3},{6,4},{7,5},{8,14},{9,15},{10,... | collective-permute-start | bytes 1179656 | tf_op jit(solution)/shard_map/ppermute | solution.py:50
  61.8 1.7 %collective-permute-start.9 = (bf16[192,512]{1,0:T(8,128)(2,1)}, bf16[192,512]{1,0:T(8,128)(2,1)S(1)}, u32[]{:S(2)}, u32[]{:S(2)}) collective-permute-start(bf16[192,512]{1,0:T(8,128)(2,1)} %get-tuple-element.52), channel_id=1, source_target_pairs={{0,1},{1,0},{2,3},{3,2},{4,5},{5,4},{6,7},{7,6},{8,9},{9,8},{10,11... | collective-permute-start | bytes 589832 | tf_op jit(solution)/shard_map/ppermute | solution.py:54
  63.6 0.9 copy-start.5
  65.1 4.3 %collective-permute-start.13 = (bf16[12,128,128]{2,1,0:T(8,128)(2,1)S(1)}, bf16[12,128,128]{2,1,0:T(8,128)(2,1)S(1)}, u32[]{:S(2)}, u32[]{:S(2)}) collective-permute-start(bf16[12,128,128]{2,1,0:T(8,128)(2,1)S(1)} %nearby.1.refs_0_), channel_id=1, source_target_pairs={{0,1},{1,0},{2,3},{3,2},{4,5},{5,4},{6,7},{7,6},{8,9},{9,8},{10,11... | collective-permute-start | bytes 1179656 | tf_op jit(solution)/shard_map/ppermute | solution.py:54
  68.9 1.7 %collective-permute-start.14 = (bf16[12,128,128]{2,1,0:T(8,128)(2,1)S(1)}, bf16[12,128,128]{2,1,0:T(8,128)(2,1)S(1)}, u32[]{:S(2)}, u32[]{:S(2)}) collective-permute-start(bf16[12,128,128]{2,1,0:T(8,128)(2,1)S(1)} %collective-permute-done.10.refs_1_), channel_id=1, source_target_pairs={{0,1},{1,0},{2,3},{3,2},{4,5},{5,4},{6,7},{7,6},{8,9},{9,8},{10,11... | collective-permute-start | bytes 1179656 | tf_op jit(solution)/shard_map/ppermute | solution.py:54
  68.9 2.3 %collective-permute-start.15 = (bf16[12,128,128]{2,1,0:T(8,128)(2,1)S(1)}, bf16[12,128,128]{2,1,0:T(8,128)(2,1)S(1)}, u32[]{:S(2)}, u32[]{:S(2)}) collective-permute-start(bf16[12,128,128]{2,1,0:T(8,128)(2,1)S(1)} %collective-permute-done.11.refs_2_), channel_id=1, source_target_pairs={{0,1},{1,0},{2,3},{3,2},{4,5},{5,4},{6,7},{7,6},{8,9},{9,8},{10,11... | collective-permute-start | bytes 1179656 | tf_op jit(solution)/shard_map/ppermute | solution.py:54
  69.4 2.3 %collective-permute-start.16 = (bf16[12,128,128]{2,1,0:T(8,128)(2,1)S(1)}, bf16[12,128,128]{2,1,0:T(8,128)(2,1)S(1)}, u32[]{:S(2)}, u32[]{:S(2)}) collective-permute-start(bf16[12,128,128]{2,1,0:T(8,128)(2,1)S(1)} %collective-permute-done.12.refs_3_), channel_id=1, source_target_pairs={{0,1},{1,0},{2,3},{3,2},{4,5},{5,4},{6,7},{7,6},{8,9},{9,8},{10,11... | collective-permute-start | bytes 1179656 | tf_op jit(solution)/shard_map/ppermute | solution.py:54
  71.8 23.6 %copy-start.1 = (bf16[4096,512]{1,0:T(8,128)(2,1)S(1)}, bf16[4096,512]{1,0:T(8,128)(2,1)}, u32[]{:S(2)}) copy-start(bf16[4096,512]{1,0:T(8,128)(2,1)} %wq_any.1) | copy-start | bytes 12582916
  87.5 3.5 %collective-permute-start.17 = (bf16[4,12,128,128]{3,2,1,0:T(8,128)(2,1)S(1)}, bf16[4,12,128,128]{3,2,1,0:T(8,128)(2,1)S(1)}, u32[]{:S(2)}, u32[]{:S(2)}) collective-permute-start(bf16[4,12,128,128]{3,2,1,0:T(8,128)(2,1)S(1)} %get-tuple-element.62), channel_id=1, source_target_pairs={{0,1},{1,0},{2,3},{3,2},{4,5},{5,4},{6,7},{7,6},{8,9},{9,8},{10,11... | collective-permute-start | bytes 4718600 | tf_op jit(solution)/shard_map/ppermute | solution.py:54
  87.7 7.7 %collective-permute-start.18 = (bf16[2,192,512]{2,1,0:T(8,128)(2,1)S(1)}, bf16[2,192,512]{2,1,0:T(8,128)(2,1)S(1)}, u32[]{:S(2)}, u32[]{:S(2)}) collective-permute-start(bf16[2,192,512]{2,1,0:T(8,128)(2,1)S(1)} %get-tuple-element.64), channel_id=1, source_target_pairs={{0,1},{1,0},{2,3},{3,2},{4,5},{5,4},{6,7},{7,6},{8,9},{9,8},{10,11... | collective-permute-start | bytes 1179656 | tf_op jit(solution)/shard_map/ppermute | solution.py:54
  91.0 4.4 %copy-start = (bf16[512,4096]{1,0:T(8,128)(2,1)S(1)}, bf16[512,4096]{1,0:T(8,128)(2,1)}, u32[]{:S(2)}) copy-start(bf16[512,4096]{1,0:T(8,128)(2,1)} %wo_any.1) | copy-start | bytes 12582916
  91.7 19.8 %collective-permute-start.21 = (bf16[12,128,128]{2,1,0:T(8,128)(2,1)S(1)}, bf16[12,128,128]{2,1,0:T(8,128)(2,1)S(1)}, u32[]{:S(2)}, u32[]{:S(2)}) collective-permute-start(bf16[12,128,128]{2,1,0:T(8,128)(2,1)S(1)} %get-tuple-element.81), channel_id=1, source_target_pairs={{0,6},{1,7},{2,0},{3,1},{4,2},{5,3},{6,4},{7,5},{8,14},{9,15},{10,... | collective-permute-start | bytes 1179656 | tf_op jit(solution)/shard_map/ppermute | solution.py:504
  94.4 17.1 %collective-permute-start.20 = (bf16[12,128,128]{2,1,0:T(8,128)(2,1)S(1)}, bf16[12,128,128]{2,1,0:T(8,128)(2,1)S(1)}, u32[]{:S(2)}, u32[]{:S(2)}) collective-permute-start(bf16[12,128,128]{2,1,0:T(8,128)(2,1)S(1)} %get-tuple-element.82), channel_id=1, source_target_pairs={{0,4},{1,5},{2,6},{3,7},{4,0},{5,1},{6,2},{7,3},{8,12},{9,13},{10,... | collective-permute-start | bytes 1179656 | tf_op jit(solution)/shard_map/ppermute | solution.py:504
  94.4 20.5 %collective-permute-start.19 = (bf16[12,128,128]{2,1,0:T(8,128)(2,1)S(1)}, bf16[12,128,128]{2,1,0:T(8,128)(2,1)S(1)}, u32[]{:S(2)}, u32[]{:S(2)}) collective-permute-start(bf16[12,128,128]{2,1,0:T(8,128)(2,1)S(1)} %get-tuple-element.83), channel_id=1, source_target_pairs={{0,2},{1,3},{2,4},{3,5},{4,6},{5,7},{6,0},{7,1},{8,10},{9,11},{10,... | collective-permute-start | bytes 1179656 | tf_op jit(solution)/shard_map/ppermute | solution.py:504
  115.0 37.5 %collective-permute-start.22 = (bf16[2,48,4096]{2,1,0:T(8,128)(2,1)}, bf16[2,48,4096]{2,1,0:T(8,128)(2,1)}, u32[]{:S(2)}, u32[]{:S(2)}) collective-permute-start(bf16[2,48,4096]{2,1,0:T(8,128)(2,1)} %get-tuple-element.70), channel_id=1, source_target_pairs={{0,2},{1,3},{2,4},{3,5},{4,6},{5,7},{6,0},{7,1},{8,10},{9,11},{10,... | collective-permute-start | bytes 2359304 | tf_op jit(solution)/shard_map/ppermute | solution.py:504
  115.0 37.5 %collective-permute-start.23 = (bf16[2,48,4096]{2,1,0:T(8,128)(2,1)}, bf16[2,48,4096]{2,1,0:T(8,128)(2,1)}, u32[]{:S(2)}, u32[]{:S(2)}) collective-permute-start(bf16[2,48,4096]{2,1,0:T(8,128)(2,1)} %get-tuple-element.71), channel_id=1, source_target_pairs={{0,4},{1,5},{2,6},{3,7},{4,0},{5,1},{6,2},{7,3},{8,12},{9,13},{10,... | collective-permute-start | bytes 2359304 | tf_op jit(solution)/shard_map/ppermute | solution.py:504
  117.3 35.8 %collective-permute-start.24 = (bf16[2,48,4096]{2,1,0:T(8,128)(2,1)S(1)}, bf16[2,48,4096]{2,1,0:T(8,128)(2,1)}, u32[]{:S(2)}, u32[]{:S(2)}) collective-permute-start(bf16[2,48,4096]{2,1,0:T(8,128)(2,1)S(1)} %get-tuple-element.72), channel_id=1, source_target_pairs={{0,6},{1,7},{2,0},{3,1},{4,2},{5,3},{6,4},{7,5},{8,14},{9,15},{10,... | collective-permute-start | bytes 2359304 | tf_op jit(solution)/shard_map/ppermute | solution.py:504
  120.8 36.5 %all-to-all-start.1 = ((bf16[32,128,128]{2,1,0:T(8,128)(2,1)}), bf16[32,128,128]{2,1,0:T(8,128)(2,1)S(1)}, u32[]{:S(2)}, u32[]{:S(2)}) async-start(bf16[32,128,128]{2,1,0:T(8,128)(2,1)} %place.1), calls=%async_computation.1 | async-start | bytes 2097152 | tf_op jit(solution)/shard_map/all_to_all | solution.py:553
  129.8 27.5 %copy-start.6 = (s32[32]{0:T(128)S(1)}, s32[32]{0:T(128)}, u32[]{:S(2)}) copy-start(s32[32]{0:T(128)} %select_reduce_fusion.slot_ref) | copy-start | bytes 388
where the time goes:
time: 159 us
  waiting for transfers between devices  54.9 us (35%)
  Pallas kernels  53.7 us (34%)
  starting transfers between devices  43.4 us (27%)
  local copies, waits for them, and re-layouts  3.22 us (2%)
  other arithmetic  2.66 us (2%)
    ppermute x6, waiting for transfers between devices, x_parts(): lax.ppermute(sums[i], 'mp', x_perm(i))  34 us
    pallas_call x1, Pallas kernels, attend(): pl.pallas_call(attend_kernel, in_specs=[SMEM] + [ANY] * 12, out_specs=[AN...  15.7 us
    pallas_call x2, Pallas kernels, project(): pl.pallas_call(functools.partial(project_kernel, cut=cut, transposed=tran...  14.7 us
    ppermute x9, starting transfers between devices, x_pieces(): lax.ppermute(block, 'mp', x_perm(-i))  13.6 us
    all_to_all x1, starting transfers between devices, body(): lax.all_to_all(outgoing, 'dp', split_axis=0, concat_axis=0, tiled=True)  11.7 us
    all_to_all x1, starting transfers between devices, body(): lax.all_to_all(place_sums(place, parts), 'dp', split_axis=0, concat_axis=...  9.04 us
    pallas_call x1, Pallas kernels, outs(): pl.pallas_call(functools.partial(outs_kernel, cut=cut), in_specs=[ANY] *...  8.8 us
    ppermute x9, waiting for transfers between devices, x_pieces(): lax.ppermute(block, 'mp', x_perm(-i))  8.09 us
  transfers between devices with their start and end apart: 27, of which 15 were waited for; matrix products, arithmetic and copies ran while one was open for 2% of the time, Pallas kernels for 23%

commit v1 on v0

--- a/solution.py
+++ b/solution.py
@@ -194,19 +194,18 @@
 
 def attend_kernel(index_ref, *refs):
     pieces = refs[:8]
-    q_any, gh_any, wk_any, wv_any, mine_any, theirs_any, keep_any, send_any = refs[8:16]
-    near, q_ref, gh_ref, wk_ref, wv_ref, small, share, sems, out_sems = refs[16:]
+    q_ref, gh_ref, wk_ref, wv_ref, mine_any, theirs_any, keep_any, send_any = refs[8:16]
+    near, small, share, sems, out_sems = refs[16:]
     neigh, depth, _ = near.shape
     cols = pieces[0].shape[2]
     groups = neigh // NBR
     keys = NBR * depth
     heads = q_ref.shape[1] // HD
     scale = 1.0 / math.sqrt(HD)
-    moves = [(wk_any, wk_ref)]
+    moves = []
     for j in range(8):
         part = pl.ds(0, NBR)
         moves.append((pieces[j].at[part], near.at[part, :, pl.ds(j * cols, cols)]))
-    moves += [(wv_any, wv_ref), (q_any, q_ref), (gh_any, gh_ref)]
     head = len(moves)
     later = pl.ds(NBR, neigh - NBR)
     for j in range(8):
@@ -289,14 +288,10 @@
     half = jax.ShapeDtypeStruct((2, length // 2, width), BF)
     return pl.pallas_call(
         attend_kernel,
-        in_specs=[SMEM] + [ANY] * 12,
+        in_specs=[SMEM] + [ANY] * 8 + [VMEM] * 4,
         out_specs=[ANY] * 4,
         scratch_shapes=[
             pltpu.VMEM((neigh, depth, 8 * cols), BF),
-            pltpu.VMEM((length, width), BF),
-            pltpu.VMEM((length, width), BF),
-            pltpu.VMEM(w_key.shape, BF),
-            pltpu.VMEM(w_value.shape, BF),
             pltpu.VMEM((2, length, width), BF),
             pltpu.VMEM((8, neigh, depth, cols), BF),
             pltpu.SemaphoreType.DMA((20,)),
@@ -415,38 +410,25 @@
     )(slot, at, table)
 
 
-def place_kernel(place_ref, *refs):
-    out_ref, total = refs[-2:]
-    at = 0
-    for i in range(0, len(refs) - 2, XS):
-        n = refs[i].shape[0]
-        acc = refs[i][...].astype(F32)
-        for r in refs[i + 1 : i + XS]:
-            acc = acc + r[...].astype(F32)
-        total[at : at + n] = acc.astype(BF)
-        at += n
-    for i in range(out_ref.shape[0]):
-        out_ref[i] = total[place_ref[i]]
-
-
-def place_sums(place, parts):
-    flat = [p for chunk in parts for p in chunk]
-    rest = flat[0].shape[1:]
-    neigh = sum(chunk[0].shape[0] for chunk in parts)
+def place_kernel(owner_ref, *refs):
+    parts, out_ref = refs[:-1], refs[-1]
+    for e in range(parts[0].shape[0]):
+        total = parts[0][e].astype(F32)
+        for part in parts[1:]:
+            total = total + part[e].astype(F32)
+        out_ref[owner_ref[e]] = total.astype(BF)
+
+
+def place_sums(owner, parts, count):
     return pl.pallas_call(
         place_kernel,
-        grid_spec=pltpu.PrefetchScalarGridSpec(
-            num_scalar_prefetch=1,
-            grid=(1,),
-            in_specs=[pl.BlockSpec(p.shape, lambda i, s: (0, 0, 0)) for p in flat],
-            out_specs=pl.BlockSpec((place.shape[0], *rest), lambda i, s: (0, 0, 0)),
-            scratch_shapes=[pltpu.VMEM((neigh, *rest), BF)],
-        ),
-        out_shape=jax.ShapeDtypeStruct((place.shape[0], *rest), BF),
+        in_specs=[SMEM] + [VMEM] * len(parts),
+        out_specs=VMEM,
+        out_shape=jax.ShapeDtypeStruct((count, *parts[0].shape[1:]), BF),
         compiler_params=params(16),
         cost_estimate=cost(0, 4 << 20),
         name="place",
-    )(place, *flat)
+    )(owner, *parts)
 
 
 def collect_kernel(slot_ref, held_ref, in_ref, out_ref):
@@ -472,23 +454,31 @@
 
 
 def final_kernel(*refs):
-    total = refs[0][...].astype(F32)
-    for r in refs[1:XS]:
-        total = total + r[...].astype(F32)
-    total = total.astype(BF)
-    refs[XS][...] = total[0]
-    refs[XS + 1][...] = total[1]
+    parts, (out0, out1, total, sems) = refs[:XS], refs[XS:]
+    cut = total.shape[2] // 4
+    copies = []
+    for k in range(4):
+        part = pl.ds(k * cut, cut)
+        sums = parts[0][:, :, part].astype(F32)
+        for r in parts[1:]:
+            sums = sums + r[:, :, part].astype(F32)
+        total[:, :, part] = sums.astype(BF)
+        for i, out in enumerate((out0, out1)):
+            src = total.at[i, :, part]
+            copies.append(pltpu.make_async_copy(src, out.at[:, part], sems.at[2 * k + i]))
+            copies[-1].start()
+    for copy in copies:
+        copy.wait()
 
 
 def final_sums(parts):
-    two, rows, full = parts[0].shape
-    cut = 1024
+    _, rows, full = parts[0].shape
     out = jax.ShapeDtypeStruct((rows, full), BF)
     return pl.pallas_call(
         final_kernel,
-        grid=(full // cut,),
-        in_specs=[pl.BlockSpec((two, rows, cut), lambda i: (0, 0, i))] * XS,
-        out_specs=[pl.BlockSpec((rows, cut), lambda i: (0, i))] * 2,
+        in_specs=[VMEM] * XS,
+        out_specs=[ANY] * 2,
+        scratch_shapes=[pltpu.VMEM(parts[0].shape, BF), pltpu.SemaphoreType.DMA((8,))],
         out_shape=[out, out],
         compiler_params=params(16),
         cost_estimate=cost(LAST << 20, 4 << 20),
@@ -521,10 +511,6 @@
     held = jnp.any(held_here, axis=1).astype(jnp.int32)
     held_slot = jnp.sum(jnp.where(held_here, slots_all, 0), axis=1).astype(jnp.int32)
     my_owners = lax.dynamic_index_in_dim(owners_all, dp_at, 0, keepdims=False)
-    place = jnp.argmax(my_owners[None, :] == jnp.arange(dp_count)[:, None], axis=1).astype(
-        jnp.int32
-    )
-
     t_own = x_pieces(tokens)
     g_own = x_pieces(grad_out)
     outgoing = choose_outgoing(held_slot, mp_at[None].astype(jnp.int32), encoded, share)
@@ -551,7 +537,7 @@
     parts2 = x_parts(after(sums2, parts))
     parts = after(parts, sums2)
     returned = lax.all_to_all(
-        place_sums(place, parts), "dp", split_axis=0, concat_axis=0, tiled=True
+        place_sums(my_owners, parts[0], dp_count), "dp", split_axis=0, concat_axis=0, tiled=True
     )
     grad_tokens, attended = final_sums(parts2)
     grad_encoded = collect(held_slot, held, after(returned, attended), encoded.shape[0])

time: 159 us -> 158 us (level)
  Pallas kernels: 53.7 us -> 51.8 us
    pallas_call x3, Pallas kernels: 21.4 us -> 19.6 us  [the longest x1 15.2 us: attend(): pl.pallas_call(attend_kernel, in_specs=[SMEM] + [ANY] * 8 + [VMEM] * 4, o...]
  transfers between devices with their start and end apart: 27 -> 27, of which waited for: 15 -> 15; matrix products, arithmetic and copies ran while one was open for 2% -> 1% of each run, Pallas kernels for 23% -> 22%
where the time goes in v1:
time: 158 us; the launch traced here: 157 us
  waiting for transfers between devices  56 us (35%)
  Pallas kernels  51.8 us (33%)
  starting transfers between devices  43.5 us (28%)
  local copies, waits for them, and re-layouts  3.17 us (2%)
  other arithmetic  1.82 us (1%)
    ppermute x6, waiting for transfers between devices, x_parts(): lax.ppermute(sums[i], 'mp', x_perm(i))  34.8 us
    pallas_call x1, Pallas kernels, attend(): pl.pallas_call(attend_kernel, in_specs=[SMEM] + [ANY] * 8 + [VMEM] * 4, o...  15.2 us
    pallas_call x2, Pallas kernels, project(): pl.pallas_call(functools.partial(project_kernel, cut=cut, transposed=tran...  14.7 us
    ppermute x9, starting transfers between devices, x_pieces(): lax.ppermute(block, 'mp', x_perm(-i))  13.6 us
    all_to_all x1, starting transfers between devices, body(): lax.all_to_all(outgoing, 'dp', split_axis=0, concat_axis=0, tiled=True)  11.7 us
    all_to_all x1, starting transfers between devices, body(): lax.all_to_all(place_sums(my_owners, parts[0], dp_count), 'dp', split_axi...  9.1 us
    pallas_call x1, Pallas kernels, outs(): pl.pallas_call(functools.partial(outs_kernel, cut=cut), in_specs=[ANY] *...  8.78 us
    ppermute x9, waiting for transfers between devices, x_pieces(): lax.ppermute(block, 'mp', x_perm(-i))  8.26 us
  transfers between devices with their start and end apart: 27, of which 15 were waited for; matrix products, arithmetic and copies ran while one was open for 1% of the time, Pallas kernels for 22%

profile of v1, /device:TPU:8, one launch (start us, length us, event | category | flops | bytes accessed | tf_op | source)
XLA Modules:
  0.0 157.3 jit_solution(18142280581129983912)
XLA Ops:
  0.6 0.1 collective-permute-start.3
  0.7 0.5 collective-permute-start.8
  1.2 3.0 %collective-permute-start.1 = (bf16[48,4096]{1,0:T(8,128)(2,1)}, bf16[48,4096]{1,0:T(8,128)(2,1)}, u32[]{:S(2)}, u32[]{:S(2)}) collective-permute-start(bf16[48,4096]{1,0:T(8,128)(2,1)} %refs_0_.1), channel_id=1, source_target_pairs={{0,4},{1,5},{2,6},{3,7},{4,0},{5,1},{6,2},{7,3},{8,12},{9,13},{10,... | collective-permute-start | bytes 1179656 | tf_op jit(solution)/shard_map/ppermute | solution.py:50
  4.3 1.1 collective-permute-start
  5.4 0.9 collective-permute-start.2
  6.3 1.3 select_reduce_fusion.slot_ref
  7.6 2.6 %outgoing.1 = bf16[32,128,128]{2,1,0:T(8,128)(2,1)} custom-call(s32[32]{0:T(128)} %select_reduce_fusion.slot_ref, s32[1]{0:T(128)} %bitcast.9.at_ref, bf16[4,128,1024]{2,1,0:T(8,128)(2,1)} %table_any.1), custom_call_target="tpu_custom_call" | custom-call | bytes 1048576 | tf_op jit(solution)/shard_map/outgoing/pallas_call | solution.py:401
  10.2 11.7 %all-to-all-start = ((bf16[32,128,128]{2,1,0:T(8,128)(2,1)}), bf16[32,128,128]{2,1,0:T(8,128)(2,1)S(1)}, u32[]{:S(2)}, u32[]{:S(2)}) async-start(bf16[32,128,128]{2,1,0:T(8,128)(2,1)} %outgoing.1), calls=%async_computation | async-start | bytes 2097152 | tf_op jit(solution)/shard_map/all_to_all | solution.py:517
  21.9 0.0 copy-start.11
  21.9 0.0 copy-start.2
  21.9 0.0 copy-start.3
  21.9 0.7 collective-permute-start.7
  22.6 0.1 collective-permute-done.refs_1_
  22.7 3.1 %collective-permute-start.6 = (bf16[48,4096]{1,0:T(8,128)(2,1)}, bf16[48,4096]{1,0:T(8,128)(2,1)}, u32[]{:S(2)}, u32[]{:S(2)}) collective-permute-start(bf16[48,4096]{1,0:T(8,128)(2,1)} %refs_0_.2), channel_id=1, source_target_pairs={{0,4},{1,5},{2,6},{3,7},{4,0},{5,1},{6,2},{7,3},{8,12},{9,13},{10,... | collective-permute-start | bytes 1179656 | tf_op jit(solution)/shard_map/ppermute | solution.py:50
  25.8 0.0 collective-permute-done.2.refs_3_
  25.8 0.9 collective-permute-start.5
  26.8 6.8 %query.1 = (bf16[192,512]{1,0:T(8,128)(2,1)}, bf16[192,512]{1,0:T(8,128)(2,1)}) custom-call(bf16[48,4096]{1,0:T(8,128)(2,1)} %refs_0_.1, bf16[48,4096]{1,0:T(8,128)(2,1)} %collective-permute-done.refs_1_, bf16[48,4096]{1,0:T(8,128)(2,1)} %collective-permute-done.1.refs_2_, bf16[48,4096]{1,0:T(8,128)(2,1)} %collective-permute-done.2.refs_3_, ...), custom_call_target="tpu_custom_call" | custom-call | flops 25769803776 | bytes 1048576 | tf_op jit(solution)/shard_map/query/pallas_call | solution.py:126
  33.6 0.1 collective-permute-start.4
  33.8 0.1 constant_dynamic-slice_fusion
  33.9 0.1 copy.13
  34.0 0.1 stack.35.index_ref
  34.1 3.4 %arrange.1 = (bf16[1024,512]{1,0:T(8,128)(2,1)S(1)}, bf16[1024,512]{1,0:T(8,128)(2,1)S(1)}) custom-call(s32[8]{0:T(128)S(1)} %stack.35.index_ref, bf16[1024,512]{1,0:T(8,128)(2,1)S(1)} %copy-done.2, bf16[1024,512]{1,0:T(8,128)(2,1)S(1)} %copy-done.3), custom_call_target="tpu_custom_call" | custom-call | bytes 1048576 | tf_op jit(solution)/shard_map/arrange/pallas_call | solution.py:160
  37.6 1.0 copy-done.7
  38.5 1.0 copy-done.9
  39.5 2.8 %collective-permute-done.6.refs_2_ = bf16[48,4096]{1,0:T(8,128)(2,1)} collective-permute-done((bf16[48,4096]{1,0:T(8,128)(2,1)}, bf16[48,4096]{1,0:T(8,128)(2,1)}, u32[]{:S(2)}, u32[]{:S(2)}) %collective-permute-start.6) | collective-permute-done | bytes 393248 | tf_op jit(solution)/shard_map/ppermute | solution.py:50
  42.3 1.7 %collective-permute-done.5.refs_1_ = bf16[48,4096]{1,0:T(8,128)(2,1)} collective-permute-done((bf16[48,4096]{1,0:T(8,128)(2,1)}, bf16[48,4096]{1,0:T(8,128)(2,1)}, u32[]{:S(2)}, u32[]{:S(2)}) %collective-permute-start.5) | collective-permute-done | bytes 393248 | tf_op jit(solution)/shard_map/ppermute | solution.py:50
  44.0 5.4 %all-to-all-done.table_ref = bf16[32,128,128]{2,1,0:T(8,128)(2,1)S(1)} async-done(((bf16[32,128,128]{2,1,0:T(8,128)(2,1)}), bf16[32,128,128]{2,1,0:T(8,128)(2,1)S(1)}, u32[]{:S(2)}, u32[]{:S(2)}) %all-to-all-start) | async-done | bytes 1048608 | tf_op jit(solution)/shard_map/all_to_all | solution.py:517
  49.4 0.0 collective-permute-done.4.refs_1_
  49.4 0.6 nearby.1.refs_0_
  50.0 0.0 copy-start.4
  50.0 0.7 collective-permute-start.12
  50.7 3.2 %collective-permute-start.11 = (bf16[12,128,128]{2,1,0:T(8,128)(2,1)S(1)}, bf16[12,128,128]{2,1,0:T(8,128)(2,1)S(1)}, u32[]{:S(2)}, u32[]{:S(2)}) collective-permute-start(bf16[12,128,128]{2,1,0:T(8,128)(2,1)S(1)} %nearby.1.refs_0_), channel_id=1, source_target_pairs={{0,4},{1,5},{2,6},{3,7},{4,0},{5,1},{6,2},{7,3},{8,12},{9,13},{10,... | collective-permute-start | bytes 1179656 | tf_op jit(solution)/shard_map/ppermute | solution.py:50
  53.9 7.8 %gheads.1 = (bf16[192,512]{1,0:T(8,128)(2,1)}, bf16[192,512]{1,0:T(8,128)(2,1)}) custom-call(bf16[48,4096]{1,0:T(8,128)(2,1)} %refs_0_.2, bf16[48,4096]{1,0:T(8,128)(2,1)} %collective-permute-done.5.refs_1_, bf16[48,4096]{1,0:T(8,128)(2,1)} %collective-permute-done.6.refs_2_, bf16[48,4096]{1,0:T(8,128)(2,1)} %collective-permute-done.7.refs_3_, ...), custom_call_target="tpu_custom_call" | custom-call | bytes 1048576 | tf_op jit(solution)/shard_map/gheads/pallas_call | solution.py:126
  61.7 0.1 collective-permute-start.9
  61.8 1.6 %collective-permute-done.9.refs_3_ = bf16[192,512]{1,0:T(8,128)(2,1)S(1)} collective-permute-done((bf16[192,512]{1,0:T(8,128)(2,1)}, bf16[192,512]{1,0:T(8,128)(2,1)S(1)}, u32[]{:S(2)}, u32[]{:S(2)}) %collective-permute-start.9) | collective-permute-done | bytes 196640 | tf_op jit(solution)/shard_map/ppermute | solution.py:54
  63.5 0.9 copy-done.5
  64.4 0.6 assemble.1
  65.0 0.2 collective-permute-start.13
  65.2 3.6 %collective-permute-done.11.refs_2_ = bf16[12,128,128]{2,1,0:T(8,128)(2,1)S(1)} collective-permute-done((bf16[12,128,128]{2,1,0:T(8,128)(2,1)S(1)}, bf16[12,128,128]{2,1,0:T(8,128)(2,1)S(1)}, u32[]{:S(2)}, u32[]{:S(2)}) %collective-permute-start.11) | collective-permute-done | bytes 393248 | tf_op jit(solution)/shard_map/ppermute | solution.py:50
  68.8 0.0 collective-permute-done.10.refs_1_
  68.9 0.5 collective-permute-start.15
  69.4 0.0 collective-permute-start.16
  69.4 1.2 collective-permute-done.14.refs_5_
  70.6 0.6 collective-permute-done.15.refs_6_
  71.1 0.6 collective-permute-done.16.refs_7_
  71.7 15.2 %attend.1 = (bf16[2,192,512]{2,1,0:T(8,128)(2,1)S(1)}, bf16[2,192,512]{2,1,0:T(8,128)(2,1)S(1)}, bf16[4,12,128,128]{3,2,1,0:T(8,128)(2,1)S(1)}, bf16[4,12,128,128]{3,2,1,0:T(8,128)(2,1)S(1)}) custom-call(s32[8]{0:T(128)S(1)} %stack.35.index_ref, bf16[12,128,128]{2,1,0:T(8,128)(2,1)S(1)} %nearby.1.refs_0_, ...), custom_call_target="tpu_custom_call" | custom-call | flops 6442450944 | bytes 1048576 | tf_op jit(solution)/shard_map/attend/pallas_call | solution.py:289
  86.9 0.2 collective-permute-start.17
  87.1 0.4 collective-permute-start.18
  87.5 2.9 %collective-permute-done.17 = bf16[4,12,128,128]{3,2,1,0:T(8,128)(2,1)S(1)} collective-permute-done((bf16[4,12,128,128]{3,2,1,0:T(8,128)(2,1)S(1)}, bf16[4,12,128,128]{3,2,1,0:T(8,128)(2,1)S(1)}, u32[]{:S(2)}, u32[]{:S(2)}) %collective-permute-start.17) | collective-permute-done | bytes 1572896 | tf_op jit(solution)/shard_map/ppermute | solution.py:54
  90.4 0.5 fusion.3
  90.9 2.7 %collective-permute-start.21 = (bf16[12,128,128]{2,1,0:T(8,128)(2,1)S(1)}, bf16[12,128,128]{2,1,0:T(8,128)(2,1)S(1)}, u32[]{:S(2)}, u32[]{:S(2)}) collective-permute-start(bf16[12,128,128]{2,1,0:T(8,128)(2,1)S(1)} %get-tuple-element.79), channel_id=1, source_target_pairs={{0,6},{1,7},{2,0},{3,1},{4,2},{5,3},{6,4},{7,5},{8,14},{9,15},{10,... | collective-permute-start | bytes 1179656 | tf_op jit(solution)/shard_map/ppermute | solution.py:494
  93.6 1.0 collective-permute-start.19
  94.6 8.8 %outs.1 = (bf16[2,48,4096]{2,1,0:T(8,128)(2,1)S(1)}, bf16[2,48,4096]{2,1,0:T(8,128)(2,1)}, bf16[2,48,4096]{2,1,0:T(8,128)(2,1)}, bf16[2,48,4096]{2,1,0:T(8,128)(2,1)S(1)}) custom-call(bf16[2,192,512]{2,1,0:T(8,128)(2,1)S(1)} %get-tuple-element.62.mine_any, bf16[2,192,512]{2,1,0:T(8,128)(2,1)S(1)} %collective-permute-done.18.got_any, ...), custom_call_target="tpu_custom_call" | custom-call | flops 966367616 | bytes 5033164 | tf_op jit(solution)/shard_map/outs/pallas_call | solution.py:348
  103.4 7.4 %collective-permute-done.21.refs_3_ = bf16[12,128,128]{2,1,0:T(8,128)(2,1)S(1)} collective-permute-done((bf16[12,128,128]{2,1,0:T(8,128)(2,1)S(1)}, bf16[12,128,128]{2,1,0:T(8,128)(2,1)S(1)}, u32[]{:S(2)}, u32[]{:S(2)}) %collective-permute-start.21) | collective-permute-done | bytes 393248 | tf_op jit(solution)/shard_map/ppermute | solution.py:494
  110.8 3.4 %collective-permute-done.19.refs_1_ = bf16[12,128,128]{2,1,0:T(8,128)(2,1)S(1)} collective-permute-done((bf16[12,128,128]{2,1,0:T(8,128)(2,1)S(1)}, bf16[12,128,128]{2,1,0:T(8,128)(2,1)S(1)}, u32[]{:S(2)}, u32[]{:S(2)}) %collective-permute-start.19) | collective-permute-done | bytes 393248 | tf_op jit(solution)/shard_map/ppermute | solution.py:494
  114.1 2.4 %collective-permute-start.23 = (bf16[2,48,4096]{2,1,0:T(8,128)(2,1)}, bf16[2,48,4096]{2,1,0:T(8,128)(2,1)}, u32[]{:S(2)}, u32[]{:S(2)}) collective-permute-start(bf16[2,48,4096]{2,1,0:T(8,128)(2,1)} %get-tuple-element.70), channel_id=1, source_target_pairs={{0,4},{1,5},{2,6},{3,7},{4,0},{5,1},{6,2},{7,3},{8,12},{9,13},{10,... | collective-permute-start | bytes 2359304 | tf_op jit(solution)/shard_map/ppermute | solution.py:494
  116.5 0.9 collective-permute-start.24
  117.4 1.7 %place.1 = bf16[32,128,128]{2,1,0:T(8,128)(2,1)} custom-call(s32[12]{0:T(128)S(1)} %bitcast.21, bf16[12,128,128]{2,1,0:T(8,128)(2,1)S(1)} %get-tuple-element.74.refs_0_, bf16[12,128,128]{2,1,0:T(8,128)(2,1)S(1)} %collective-permute-done.19.refs_1_, bf16[12,128,128]{2,1,0:T(8,128)(2,1)S(1)} %collective-permute-done.20.refs_2_, ...), custom_call_target="tpu_custom_call" | custom-call | bytes 4194304 | tf_op jit(solution)/shard_map/place/pallas_call | solution.py:423
  119.1 9.1 %all-to-all-start.1 = ((bf16[32,128,128]{2,1,0:T(8,128)(2,1)}), bf16[32,128,128]{2,1,0:T(8,128)(2,1)S(1)}, u32[]{:S(2)}, u32[]{:S(2)}) async-start(bf16[32,128,128]{2,1,0:T(8,128)(2,1)} %place.1), calls=%async_computation.1 | async-start | bytes 2097152 | tf_op jit(solution)/shard_map/all_to_all | solution.py:539
  128.3 23.4 %collective-permute-done.22.refs_1_ = bf16[2,48,4096]{2,1,0:T(8,128)(2,1)} collective-permute-done((bf16[2,48,4096]{2,1,0:T(8,128)(2,1)}, bf16[2,48,4096]{2,1,0:T(8,128)(2,1)}, u32[]{:S(2)}, u32[]{:S(2)}) %collective-permute-start.22) | collective-permute-done | bytes 786464 | tf_op jit(solution)/shard_map/ppermute | solution.py:494
  151.7 0.6 collective-permute-done.24.refs_3_
  152.3 2.7 %final.1 = (bf16[48,4096]{1,0:T(8,128)(2,1)}, bf16[48,4096]{1,0:T(8,128)(2,1)}) custom-call(bf16[2,48,4096]{2,1,0:T(8,128)(2,1)S(1)} %get-tuple-element.68.refs_0_, bf16[2,48,4096]{2,1,0:T(8,128)(2,1)} %collective-permute-done.22.refs_1_, bf16[2,48,4096]{2,1,0:T(8,128)(2,1)} %collective-permute-done.23.refs_2_, ...), custom_call_target="tpu_custom_call" | custom-call | flops 68719476736 | bytes 4194304 | tf_op jit(solution)/shard_map/final/pallas_call | solution.py:477
  155.1 0.7 all-to-all-done.1.in_ref
  155.8 1.5 collect.1
  (33 shorter events, 0.1 us)
Async XLA Ops:
  0.6 26.1 %collective-permute-start.3 = (bf16[4096,512]{1,0:T(8,128)(2,1)}, bf16[4096,512]{1,0:T(8,128)(2,1)}, u32[]{:S(2)}, u32[]{:S(2)}) collective-permute-start(bf16[4096,512]{1,0:T(8,128)(2,1)} %wq_any.1), channel_id=1, source_target_pairs={{0,1},{1,0},{2,3},{3,2},{4,5},{5,4},{6,7},{7,6},{8,9},{9,8},{10,11... | collective-permute-start | bytes 12582920 | tf_op jit(solution)/shard_map/ppermute | solution.py:54
  0.7 53.2 %collective-permute-start.8 = (bf16[512,4096]{1,0:T(8,128)(2,1)}, bf16[512,4096]{1,0:T(8,128)(2,1)}, u32[]{:S(2)}, u32[]{:S(2)}) collective-permute-start(bf16[512,4096]{1,0:T(8,128)(2,1)} %wo_any.1), channel_id=1, source_target_pairs={{0,1},{1,0},{2,3},{3,2},{4,5},{5,4},{6,7},{7,6},{8,9},{9,8},{10,11... | collective-permute-start | bytes 12582920 | tf_op jit(solution)/shard_map/ppermute | solution.py:54
  1.2 20.7 %collective-permute-start.1 = (bf16[48,4096]{1,0:T(8,128)(2,1)}, bf16[48,4096]{1,0:T(8,128)(2,1)}, u32[]{:S(2)}, u32[]{:S(2)}) collective-permute-start(bf16[48,4096]{1,0:T(8,128)(2,1)} %refs_0_.1), channel_id=1, source_target_pairs={{0,4},{1,5},{2,6},{3,7},{4,0},{5,1},{6,2},{7,3},{8,12},{9,13},{10,... | collective-permute-start | bytes 1179656 | tf_op jit(solution)/shard_map/ppermute | solution.py:50
  4.3 18.5 %collective-permute-start = (bf16[48,4096]{1,0:T(8,128)(2,1)}, bf16[48,4096]{1,0:T(8,128)(2,1)}, u32[]{:S(2)}, u32[]{:S(2)}) collective-permute-start(bf16[48,4096]{1,0:T(8,128)(2,1)} %refs_0_.1), channel_id=1, source_target_pairs={{0,6},{1,7},{2,0},{3,1},{4,2},{5,3},{6,4},{7,5},{8,14},{9,15},{10,... | collective-permute-start | bytes 1179656 | tf_op jit(solution)/shard_map/ppermute | solution.py:50
  5.4 20.4 %collective-permute-start.2 = (bf16[48,4096]{1,0:T(8,128)(2,1)}, bf16[48,4096]{1,0:T(8,128)(2,1)}, u32[]{:S(2)}, u32[]{:S(2)}) collective-permute-start(bf16[48,4096]{1,0:T(8,128)(2,1)} %refs_0_.1), channel_id=1, source_target_pairs={{0,2},{1,3},{2,4},{3,5},{4,6},{5,7},{6,0},{7,1},{8,10},{9,11},{10,... | collective-permute-start | bytes 1179656 | tf_op jit(solution)/shard_map/ppermute | solution.py:50
  10.2 39.2 %all-to-all-start = ((bf16[32,128,128]{2,1,0:T(8,128)(2,1)}), bf16[32,128,128]{2,1,0:T(8,128)(2,1)S(1)}, u32[]{:S(2)}, u32[]{:S(2)}) async-start(bf16[32,128,128]{2,1,0:T(8,128)(2,1)} %outgoing.1), calls=%async_computation | async-start | bytes 2097152 | tf_op jit(solution)/shard_map/all_to_all | solution.py:517
  21.9 11.9 %copy-start.11 = (s32[32,6,2]{0,2,1:T(2,128)S(1)}, s32[32,6,2]{0,2,1:T(2,128)}, u32[]{:S(2)}) copy-start(s32[32,6,2]{0,2,1:T(2,128)} %param.11) | copy-start | bytes 4612
  21.9 12.2 %copy-start.2 = (bf16[1024,512]{1,0:T(8,128)(2,1)S(1)}, bf16[1024,512]{1,0:T(8,128)(2,1)}, u32[]{:S(2)}) copy-start(bf16[1024,512]{1,0:T(8,128)(2,1)} %wk_any) | copy-start | bytes 3145732
  21.9 12.2 %copy-start.3 = (bf16[1024,512]{1,0:T(8,128)(2,1)S(1)}, bf16[1024,512]{1,0:T(8,128)(2,1)}, u32[]{:S(2)}) copy-start(bf16[1024,512]{1,0:T(8,128)(2,1)} %wv_any.1) | copy-start | bytes 3145732
  21.9 17.6 %collective-permute-start.7 = (bf16[48,4096]{1,0:T(8,128)(2,1)}, bf16[48,4096]{1,0:T(8,128)(2,1)}, u32[]{:S(2)}, u32[]{:S(2)}) collective-permute-start(bf16[48,4096]{1,0:T(8,128)(2,1)} %refs_0_.2), channel_id=1, source_target_pairs={{0,2},{1,3},{2,4},{3,5},{4,6},{5,7},{6,0},{7,1},{8,10},{9,11},{10,... | collective-permute-start | bytes 1179656 | tf_op jit(solution)/shard_map/ppermute | solution.py:50
  22.7 19.5 %collective-permute-start.6 = (bf16[48,4096]{1,0:T(8,128)(2,1)}, bf16[48,4096]{1,0:T(8,128)(2,1)}, u32[]{:S(2)}, u32[]{:S(2)}) collective-permute-start(bf16[48,4096]{1,0:T(8,128)(2,1)} %refs_0_.2), channel_id=1, source_target_pairs={{0,4},{1,5},{2,6},{3,7},{4,0},{5,1},{6,2},{7,3},{8,12},{9,13},{10,... | collective-permute-start | bytes 1179656 | tf_op jit(solution)/shard_map/ppermute | solution.py:50
  25.8 18.2 %collective-permute-start.5 = (bf16[48,4096]{1,0:T(8,128)(2,1)}, bf16[48,4096]{1,0:T(8,128)(2,1)}, u32[]{:S(2)}, u32[]{:S(2)}) collective-permute-start(bf16[48,4096]{1,0:T(8,128)(2,1)} %refs_0_.2), channel_id=1, source_target_pairs={{0,6},{1,7},{2,0},{3,1},{4,2},{5,3},{6,4},{7,5},{8,14},{9,15},{10,... | collective-permute-start | bytes 1179656 | tf_op jit(solution)/shard_map/ppermute | solution.py:50
  33.6 15.8 %collective-permute-start.4 = (bf16[192,512]{1,0:T(8,128)(2,1)}, bf16[192,512]{1,0:T(8,128)(2,1)S(1)}, u32[]{:S(2)}, u32[]{:S(2)}) collective-permute-start(bf16[192,512]{1,0:T(8,128)(2,1)} %get-tuple-element.42), channel_id=1, source_target_pairs={{0,1},{1,0},{2,3},{3,2},{4,5},{5,4},{6,7},{7,6},{8,9},{9,8},{10,11... | collective-permute-start | bytes 589832 | tf_op jit(solution)/shard_map/ppermute | solution.py:54
  37.6 1.0 copy-start.7
  38.5 1.0 copy-start.9
  50.0 13.5 %copy-start.4 = (bf16[192,512]{1,0:T(8,128)(2,1)S(1)}, bf16[192,512]{1,0:T(8,128)(2,1)}, u32[]{:S(2)}) copy-start(bf16[192,512]{1,0:T(8,128)(2,1)} %get-tuple-element.41.refs_0_) | copy-start | bytes 589828
  50.0 21.7 %copy-start.8 = (bf16[1024,512]{1,0:T(8,128)(2,1)S(1)}, bf16[1024,512]{1,0:T(8,128)(2,1)}, u32[]{:S(2)}) copy-start(bf16[1024,512]{1,0:T(8,128)(2,1)} %copy-done.7) | copy-start | bytes 3145732
  50.0 21.7 %copy-start.10 = (bf16[1024,512]{1,0:T(8,128)(2,1)S(1)}, bf16[1024,512]{1,0:T(8,128)(2,1)}, u32[]{:S(2)}) copy-start(bf16[1024,512]{1,0:T(8,128)(2,1)} %copy-done.9) | copy-start | bytes 3145732
  50.0 15.2 %collective-permute-start.12 = (bf16[12,128,128]{2,1,0:T(8,128)(2,1)S(1)}, bf16[12,128,128]{2,1,0:T(8,128)(2,1)S(1)}, u32[]{:S(2)}, u32[]{:S(2)}) collective-permute-start(bf16[12,128,128]{2,1,0:T(8,128)(2,1)S(1)} %nearby.1.refs_0_), channel_id=1, source_target_pairs={{0,2},{1,3},{2,4},{3,5},{4,6},{5,7},{6,0},{7,1},{8,10},{9,11},{10,... | collective-permute-start | bytes 1179656 | tf_op jit(solution)/shard_map/ppermute | solution.py:50
  50.7 18.1 %collective-permute-start.11 = (bf16[12,128,128]{2,1,0:T(8,128)(2,1)S(1)}, bf16[12,128,128]{2,1,0:T(8,128)(2,1)S(1)}, u32[]{:S(2)}, u32[]{:S(2)}) collective-permute-start(bf16[12,128,128]{2,1,0:T(8,128)(2,1)S(1)} %nearby.1.refs_0_), channel_id=1, source_target_pairs={{0,4},{1,5},{2,6},{3,7},{4,0},{5,1},{6,2},{7,3},{8,12},{9,13},{10,... | collective-permute-start | bytes 1179656 | tf_op jit(solution)/shard_map/ppermute | solution.py:50
  53.9 15.0 %collective-permute-start.10 = (bf16[12,128,128]{2,1,0:T(8,128)(2,1)S(1)}, bf16[12,128,128]{2,1,0:T(8,128)(2,1)S(1)}, u32[]{:S(2)}, u32[]{:S(2)}) collective-permute-start(bf16[12,128,128]{2,1,0:T(8,128)(2,1)S(1)} %nearby.1.refs_0_), channel_id=1, source_target_pairs={{0,6},{1,7},{2,0},{3,1},{4,2},{5,3},{6,4},{7,5},{8,14},{9,15},{10,... | collective-permute-start | bytes 1179656 | tf_op jit(solution)/shard_map/ppermute | solution.py:50
  61.7 1.7 %collective-permute-start.9 = (bf16[192,512]{1,0:T(8,128)(2,1)}, bf16[192,512]{1,0:T(8,128)(2,1)S(1)}, u32[]{:S(2)}, u32[]{:S(2)}) collective-permute-start(bf16[192,512]{1,0:T(8,128)(2,1)} %get-tuple-element.51), channel_id=1, source_target_pairs={{0,1},{1,0},{2,3},{3,2},{4,5},{5,4},{6,7},{7,6},{8,9},{9,8},{10,11... | collective-permute-start | bytes 589832 | tf_op jit(solution)/shard_map/ppermute | solution.py:54
  63.5 0.9 copy-start.5
  65.0 4.4 %collective-permute-start.13 = (bf16[12,128,128]{2,1,0:T(8,128)(2,1)S(1)}, bf16[12,128,128]{2,1,0:T(8,128)(2,1)S(1)}, u32[]{:S(2)}, u32[]{:S(2)}) collective-permute-start(bf16[12,128,128]{2,1,0:T(8,128)(2,1)S(1)} %nearby.1.refs_0_), channel_id=1, source_target_pairs={{0,1},{1,0},{2,3},{3,2},{4,5},{5,4},{6,7},{7,6},{8,9},{9,8},{10,11... | collective-permute-start | bytes 1179656 | tf_op jit(solution)/shard_map/ppermute | solution.py:54
  68.9 1.7 %collective-permute-start.14 = (bf16[12,128,128]{2,1,0:T(8,128)(2,1)S(1)}, bf16[12,128,128]{2,1,0:T(8,128)(2,1)S(1)}, u32[]{:S(2)}, u32[]{:S(2)}) collective-permute-start(bf16[12,128,128]{2,1,0:T(8,128)(2,1)S(1)} %collective-permute-done.10.refs_1_), channel_id=1, source_target_pairs={{0,1},{1,0},{2,3},{3,2},{4,5},{5,4},{6,7},{7,6},{8,9},{9,8},{10,11... | collective-permute-start | bytes 1179656 | tf_op jit(solution)/shard_map/ppermute | solution.py:54
  68.9 2.3 %collective-permute-start.15 = (bf16[12,128,128]{2,1,0:T(8,128)(2,1)S(1)}, bf16[12,128,128]{2,1,0:T(8,128)(2,1)S(1)}, u32[]{:S(2)}, u32[]{:S(2)}) collective-permute-start(bf16[12,128,128]{2,1,0:T(8,128)(2,1)S(1)} %collective-permute-done.11.refs_2_), channel_id=1, source_target_pairs={{0,1},{1,0},{2,3},{3,2},{4,5},{5,4},{6,7},{7,6},{8,9},{9,8},{10,11... | collective-permute-start | bytes 1179656 | tf_op jit(solution)/shard_map/ppermute | solution.py:54
  69.4 2.3 %collective-permute-start.16 = (bf16[12,128,128]{2,1,0:T(8,128)(2,1)S(1)}, bf16[12,128,128]{2,1,0:T(8,128)(2,1)S(1)}, u32[]{:S(2)}, u32[]{:S(2)}) collective-permute-start(bf16[12,128,128]{2,1,0:T(8,128)(2,1)S(1)} %collective-permute-done.12.refs_3_), channel_id=1, source_target_pairs={{0,1},{1,0},{2,3},{3,2},{4,5},{5,4},{6,7},{7,6},{8,9},{9,8},{10,11... | collective-permute-start | bytes 1179656 | tf_op jit(solution)/shard_map/ppermute | solution.py:54
  71.7 22.9 %copy-start.1 = (bf16[4096,512]{1,0:T(8,128)(2,1)S(1)}, bf16[4096,512]{1,0:T(8,128)(2,1)}, u32[]{:S(2)}) copy-start(bf16[4096,512]{1,0:T(8,128)(2,1)} %wq_any.1) | copy-start | bytes 12582916
  86.9 3.5 %collective-permute-start.17 = (bf16[4,12,128,128]{3,2,1,0:T(8,128)(2,1)S(1)}, bf16[4,12,128,128]{3,2,1,0:T(8,128)(2,1)S(1)}, u32[]{:S(2)}, u32[]{:S(2)}) collective-permute-start(bf16[4,12,128,128]{3,2,1,0:T(8,128)(2,1)S(1)} %get-tuple-element.61), channel_id=1, source_target_pairs={{0,1},{1,0},{2,3},{3,2},{4,5},{5,4},{6,7},{7,6},{8,9},{9,8},{10,11... | collective-permute-start | bytes 4718600 | tf_op jit(solution)/shard_map/ppermute | solution.py:54
  87.1 7.5 %collective-permute-start.18 = (bf16[2,192,512]{2,1,0:T(8,128)(2,1)S(1)}, bf16[2,192,512]{2,1,0:T(8,128)(2,1)S(1)}, u32[]{:S(2)}, u32[]{:S(2)}) collective-permute-start(bf16[2,192,512]{2,1,0:T(8,128)(2,1)S(1)} %get-tuple-element.63), channel_id=1, source_target_pairs={{0,1},{1,0},{2,3},{3,2},{4,5},{5,4},{6,7},{7,6},{8,9},{9,8},{10,11... | collective-permute-start | bytes 1179656 | tf_op jit(solution)/shard_map/ppermute | solution.py:54
  90.4 4.2 %copy-start = (bf16[512,4096]{1,0:T(8,128)(2,1)S(1)}, bf16[512,4096]{1,0:T(8,128)(2,1)}, u32[]{:S(2)}) copy-start(bf16[512,4096]{1,0:T(8,128)(2,1)} %wo_any.1) | copy-start | bytes 12582916
  90.9 19.8 %collective-permute-start.21 = (bf16[12,128,128]{2,1,0:T(8,128)(2,1)S(1)}, bf16[12,128,128]{2,1,0:T(8,128)(2,1)S(1)}, u32[]{:S(2)}, u32[]{:S(2)}) collective-permute-start(bf16[12,128,128]{2,1,0:T(8,128)(2,1)S(1)} %get-tuple-element.79), channel_id=1, source_target_pairs={{0,6},{1,7},{2,0},{3,1},{4,2},{5,3},{6,4},{7,5},{8,14},{9,15},{10,... | collective-permute-start | bytes 1179656 | tf_op jit(solution)/shard_map/ppermute | solution.py:494
  93.6 17.1 %collective-permute-start.20 = (bf16[12,128,128]{2,1,0:T(8,128)(2,1)S(1)}, bf16[12,128,128]{2,1,0:T(8,128)(2,1)S(1)}, u32[]{:S(2)}, u32[]{:S(2)}) collective-permute-start(bf16[12,128,128]{2,1,0:T(8,128)(2,1)S(1)} %get-tuple-element.80), channel_id=1, source_target_pairs={{0,4},{1,5},{2,6},{3,7},{4,0},{5,1},{6,2},{7,3},{8,12},{9,13},{10,... | collective-permute-start | bytes 1179656 | tf_op jit(solution)/shard_map/ppermute | solution.py:494
  93.6 20.5 %collective-permute-start.19 = (bf16[12,128,128]{2,1,0:T(8,128)(2,1)S(1)}, bf16[12,128,128]{2,1,0:T(8,128)(2,1)S(1)}, u32[]{:S(2)}, u32[]{:S(2)}) collective-permute-start(bf16[12,128,128]{2,1,0:T(8,128)(2,1)S(1)} %get-tuple-element.81), channel_id=1, source_target_pairs={{0,2},{1,3},{2,4},{3,5},{4,6},{5,7},{6,0},{7,1},{8,10},{9,11},{10,... | collective-permute-start | bytes 1179656 | tf_op jit(solution)/shard_map/ppermute | solution.py:494
  114.1 37.5 %collective-permute-start.22 = (bf16[2,48,4096]{2,1,0:T(8,128)(2,1)}, bf16[2,48,4096]{2,1,0:T(8,128)(2,1)}, u32[]{:S(2)}, u32[]{:S(2)}) collective-permute-start(bf16[2,48,4096]{2,1,0:T(8,128)(2,1)} %get-tuple-element.69), channel_id=1, source_target_pairs={{0,2},{1,3},{2,4},{3,5},{4,6},{5,7},{6,0},{7,1},{8,10},{9,11},{10,... | collective-permute-start | bytes 2359304 | tf_op jit(solution)/shard_map/ppermute | solution.py:494
  114.1 37.5 %collective-permute-start.23 = (bf16[2,48,4096]{2,1,0:T(8,128)(2,1)}, bf16[2,48,4096]{2,1,0:T(8,128)(2,1)}, u32[]{:S(2)}, u32[]{:S(2)}) collective-permute-start(bf16[2,48,4096]{2,1,0:T(8,128)(2,1)} %get-tuple-element.70), channel_id=1, source_target_pairs={{0,4},{1,5},{2,6},{3,7},{4,0},{5,1},{6,2},{7,3},{8,12},{9,13},{10,... | collective-permute-start | bytes 2359304 | tf_op jit(solution)/shard_map/ppermute | solution.py:494
  116.5 35.8 %collective-permute-start.24 = (bf16[2,48,4096]{2,1,0:T(8,128)(2,1)S(1)}, bf16[2,48,4096]{2,1,0:T(8,128)(2,1)}, u32[]{:S(2)}, u32[]{:S(2)}) collective-permute-start(bf16[2,48,4096]{2,1,0:T(8,128)(2,1)S(1)} %get-tuple-element.71), channel_id=1, source_target_pairs={{0,6},{1,7},{2,0},{3,1},{4,2},{5,3},{6,4},{7,5},{8,14},{9,15},{10,... | collective-permute-start | bytes 2359304 | tf_op jit(solution)/shard_map/ppermute | solution.py:494
  119.1 36.6 %all-to-all-start.1 = ((bf16[32,128,128]{2,1,0:T(8,128)(2,1)}), bf16[32,128,128]{2,1,0:T(8,128)(2,1)S(1)}, u32[]{:S(2)}, u32[]{:S(2)}) async-start(bf16[32,128,128]{2,1,0:T(8,128)(2,1)} %place.1), calls=%async_computation.1 | async-start | bytes 2097152 | tf_op jit(solution)/shard_map/all_to_all | solution.py:539
  128.3 27.5 %copy-start.6 = (s32[32]{0:T(128)S(1)}, s32[32]{0:T(128)}, u32[]{:S(2)}) copy-start(s32[32]{0:T(128)} %select_reduce_fusion.slot_ref) | copy-start | bytes 388

commit v2 on v1

--- a/solution.py
+++ b/solution.py
@@ -17,7 +17,7 @@
 F32 = jnp.float32
 BIG = 56
 B_PROJ = 56
-B_ATT = 40
+B_ATT = 30
 B_OUTS = 30
 FIRST = 16
 OUTS = 0.3
@@ -194,44 +194,19 @@
 
 def attend_kernel(index_ref, *refs):
     pieces = refs[:8]
-    q_ref, gh_ref, wk_ref, wv_ref, mine_any, theirs_any, keep_any, send_any = refs[8:16]
-    near, small, share, sems, out_sems = refs[16:]
-    neigh, depth, _ = near.shape
-    cols = pieces[0].shape[2]
+    q_ref, gh_ref, wk_ref, wv_ref, mine_ref, theirs_ref, keep_ref, send_ref, small = refs[8:]
+    neigh, depth, cols = pieces[0].shape
     groups = neigh // NBR
     keys = NBR * depth
     heads = q_ref.shape[1] // HD
     scale = 1.0 / math.sqrt(HD)
-    moves = []
-    for j in range(8):
-        part = pl.ds(0, NBR)
-        moves.append((pieces[j].at[part], near.at[part, :, pl.ds(j * cols, cols)]))
-    head = len(moves)
-    later = pl.ds(NBR, neigh - NBR)
-    for j in range(8):
-        moves.append((pieces[j].at[later], near.at[later, :, pl.ds(j * cols, cols)]))
-    copies = [pltpu.make_async_copy(s, d, sems.at[i]) for i, (s, d) in enumerate(moves)]
-    for copy in copies:
-        copy.start()
     part = [slice(h * HD, (h + 1) * HD) for h in range(heads)]
-
-    def stores(g):
-        two = pl.ds(g * NBR, NBR)
-        return [
-            pltpu.make_async_copy(share.at[pl.ds(0, XS), two], keep_any.at[:, two], out_sems.at[2 * g]),
-            pltpu.make_async_copy(share.at[pl.ds(XS, XS), two], send_any.at[:, two], out_sems.at[2 * g + 1]),
-        ]
 
     def group(g, _):
         own = pl.ds(pl.multiple_of(g * GROUP, GROUP), GROUP)
         two = pl.ds(g * NBR, NBR)
 
-        @pl.when(g == 1)
-        def _():
-            for copy in copies[head:]:
-                copy.wait()
-
-        near_rows = near[two].reshape(keys, near.shape[2])
+        near_rows = jnp.concatenate([p[two].reshape(keys, cols) for p in pieces], axis=1)
         k = mm(near_rows, wk_ref[...]).astype(BF)
         v = mm(near_rows, wv_ref[...]).astype(BF)
         q = q_ref[own, :]
@@ -256,47 +231,29 @@
         for j in range(0, 8, 2):
             put = slice(j * cols, (j + 2) * cols)
             grad = (mm_nt(gk, wk_ref[put, :]) + mm_nt(gv, wv_ref[put, :])).astype(BF)
-            share[j, two] = grad[:, :cols].reshape(NBR, depth, cols)
-            share[j + 1, two] = grad[:, cols:].reshape(NBR, depth, cols)
-        for copy in stores(g):
-            copy.start()
+            for i in range(2):
+                ref = (keep_ref, send_ref)[(j + i) // XS]
+                ref[(j + i) % XS, two] = grad[:, i * cols : (i + 1) * cols].reshape(NBR, depth, cols)
         return 0
 
-    for copy in copies[:head]:
-        copy.wait()
-    lax.fori_loop(0, groups, group, 0)
+    lax.fori_loop(0, groups, group, 0, unroll=2)
     rows = small.shape[1] // 8
-    last = []
     for j in range(8):
         at = pl.ds(pl.multiple_of(index_ref[j] * rows, 16), rows)
-        put = pl.ds(j % XS * rows, rows)
-        dst = (mine_any, theirs_any)[j // XS].at[:, put, :]
-        last.append(pltpu.make_async_copy(small.at[:, at, :], dst, out_sems.at[2 * groups + j]))
-        last[-1].start()
-    for g in range(groups):
-        for copy in stores(g):
-            copy.wait()
-    for copy in last:
-        copy.wait()
+        put = slice(j % XS * rows, (j % XS + 1) * rows)
+        (mine_ref, theirs_ref)[j // XS][:, put, :] = small[:, at, :]
 
 
 def attend(indices, pieces, q, gh, w_key, w_value):
     neigh, depth, cols = pieces[0].shape
     length, width = q.shape
-    groups = neigh // NBR
     share = jax.ShapeDtypeStruct((XS, neigh, depth, cols), BF)
     half = jax.ShapeDtypeStruct((2, length // 2, width), BF)
     return pl.pallas_call(
         attend_kernel,
-        in_specs=[SMEM] + [ANY] * 8 + [VMEM] * 4,
-        out_specs=[ANY] * 4,
-        scratch_shapes=[
-            pltpu.VMEM((neigh, depth, 8 * cols), BF),
-            pltpu.VMEM((2, length, width), BF),
-            pltpu.VMEM((8, neigh, depth, cols), BF),
-            pltpu.SemaphoreType.DMA((20,)),
-            pltpu.SemaphoreType.DMA((2 * groups + 8,)),
-        ],
+        in_specs=[SMEM] + [VMEM] * 12,
+        out_specs=[VMEM] * 4,
+        scratch_shapes=[pltpu.VMEM((2, length, width), BF)],
         out_shape=[half, half, share, share],
         compiler_params=params(B_ATT),
         cost_estimate=cost(int(ATT * 8 * neigh * depth * 8 * cols * width), 1 << 20),

time: 158 us -> 155 us (0.981)
  Pallas kernels: 51.8 us -> 48.9 us
    pallas_call x1, Pallas kernels: 15.2 us -> 12.2 us  [attend(): pl.pallas_call(attend_kernel, in_specs=[SMEM] + [VMEM] * 12, out_specs=[V...]
  transfers between devices with their start and end apart: 27 -> 27, of which waited for: 15 -> 15; matrix products, arithmetic and copies ran while one was open for 1% -> 1% of each run, Pallas kernels for 22% -> 23%
where the time goes in v2:
time: 155 us; the launch traced here: 154 us
  waiting for transfers between devices  56 us (36%)
  Pallas kernels  48.9 us (32%)
  starting transfers between devices  43.5 us (28%)
  local copies, waits for them, and re-layouts  3.17 us (2%)
  other arithmetic  1.98 us (1%)
    ppermute x6, waiting for transfers between devices, x_parts(): lax.ppermute(sums[i], 'mp', x_perm(i))  34.8 us
    pallas_call x2, Pallas kernels, project(): pl.pallas_call(functools.partial(project_kernel, cut=cut, transposed=tran...  14.7 us
    ppermute x9, starting transfers between devices, x_pieces(): lax.ppermute(block, 'mp', x_perm(-i))  13.6 us
    pallas_call x1, Pallas kernels, attend(): pl.pallas_call(attend_kernel, in_specs=[SMEM] + [VMEM] * 12, out_specs=[V...  12.2 us
    all_to_all x1, starting transfers between devices, body(): lax.all_to_all(outgoing, 'dp', split_axis=0, concat_axis=0, tiled=True)  11.7 us
    all_to_all x1, starting transfers between devices, body(): lax.all_to_all(place_sums(my_owners, parts[0], dp_count), 'dp', split_axi...  9.1 us
    pallas_call x1, Pallas kernels, outs(): pl.pallas_call(functools.partial(outs_kernel, cut=cut), in_specs=[ANY] *...  8.78 us
    ppermute x9, waiting for transfers between devices, x_pieces(): lax.ppermute(block, 'mp', x_perm(-i))  8.26 us
  transfers between devices with their start and end apart: 27, of which 15 were waited for; matrix products, arithmetic and copies ran while one was open for 1% of the time, Pallas kernels for 23%

profile of v2, /device:TPU:8, one launch (start us, length us, event | category | flops | bytes accessed | tf_op | source)
XLA Modules:
  0.0 154.5 jit_solution(8062873123765017151)
XLA Ops:
  0.6 0.1 collective-permute-start.3
  0.7 0.5 collective-permute-start.8
  1.2 3.0 %collective-permute-start.1 = (bf16[48,4096]{1,0:T(8,128)(2,1)}, bf16[48,4096]{1,0:T(8,128)(2,1)}, u32[]{:S(2)}, u32[]{:S(2)}) collective-permute-start(bf16[48,4096]{1,0:T(8,128)(2,1)} %refs_0_.1), channel_id=1, source_target_pairs={{0,4},{1,5},{2,6},{3,7},{4,0},{5,1},{6,2},{7,3},{8,12},{9,13},{10,... | collective-permute-start | bytes 1179656 | tf_op jit(solution)/shard_map/ppermute | solution.py:50
  4.3 1.1 collective-permute-start
  5.4 0.9 collective-permute-start.2
  6.3 1.3 select_reduce_fusion.slot_ref
  7.6 2.6 %outgoing.1 = bf16[32,128,128]{2,1,0:T(8,128)(2,1)} custom-call(s32[32]{0:T(128)} %select_reduce_fusion.slot_ref, s32[1]{0:T(128)} %bitcast.9.at_ref, bf16[4,128,1024]{2,1,0:T(8,128)(2,1)} %table_any.1), custom_call_target="tpu_custom_call" | custom-call | bytes 1048576 | tf_op jit(solution)/shard_map/outgoing/pallas_call | solution.py:358
  10.2 11.7 %all-to-all-start = ((bf16[32,128,128]{2,1,0:T(8,128)(2,1)}), bf16[32,128,128]{2,1,0:T(8,128)(2,1)S(1)}, u32[]{:S(2)}, u32[]{:S(2)}) async-start(bf16[32,128,128]{2,1,0:T(8,128)(2,1)} %outgoing.1), calls=%async_computation | async-start | bytes 2097152 | tf_op jit(solution)/shard_map/all_to_all | solution.py:474
  21.9 0.0 copy-start.11
  21.9 0.0 copy-start.2
  21.9 0.0 copy-start.3
  21.9 0.0 collective-permute-done.1.refs_2_
  21.9 0.7 collective-permute-start.7
  22.6 0.1 collective-permute-done.refs_1_
  22.7 3.1 %collective-permute-start.6 = (bf16[48,4096]{1,0:T(8,128)(2,1)}, bf16[48,4096]{1,0:T(8,128)(2,1)}, u32[]{:S(2)}, u32[]{:S(2)}) collective-permute-start(bf16[48,4096]{1,0:T(8,128)(2,1)} %refs_0_.2), channel_id=1, source_target_pairs={{0,4},{1,5},{2,6},{3,7},{4,0},{5,1},{6,2},{7,3},{8,12},{9,13},{10,... | collective-permute-start | bytes 1179656 | tf_op jit(solution)/shard_map/ppermute | solution.py:50
  25.8 0.0 collective-permute-done.2.refs_3_
  25.8 0.9 collective-permute-start.5
  26.8 6.8 %query.1 = (bf16[192,512]{1,0:T(8,128)(2,1)}, bf16[192,512]{1,0:T(8,128)(2,1)}) custom-call(bf16[48,4096]{1,0:T(8,128)(2,1)} %refs_0_.1, bf16[48,4096]{1,0:T(8,128)(2,1)} %collective-permute-done.refs_1_, bf16[48,4096]{1,0:T(8,128)(2,1)} %collective-permute-done.1.refs_2_, bf16[48,4096]{1,0:T(8,128)(2,1)} %collective-permute-done.2.refs_3_, ...), custom_call_target="tpu_custom_call" | custom-call | flops 25769803776 | bytes 1048576 | tf_op jit(solution)/shard_map/query/pallas_call | solution.py:126
  33.6 0.1 collective-permute-start.4
  33.8 0.1 constant_dynamic-slice_fusion
  33.9 0.1 copy.13
  34.0 0.1 stack.35.index_ref
  34.1 3.4 %arrange.1 = (bf16[1024,512]{1,0:T(8,128)(2,1)S(1)}, bf16[1024,512]{1,0:T(8,128)(2,1)S(1)}) custom-call(s32[8]{0:T(128)S(1)} %stack.35.index_ref, bf16[1024,512]{1,0:T(8,128)(2,1)S(1)} %copy-done.2, bf16[1024,512]{1,0:T(8,128)(2,1)S(1)} %copy-done.3), custom_call_target="tpu_custom_call" | custom-call | bytes 1048576 | tf_op jit(solution)/shard_map/arrange/pallas_call | solution.py:160
  37.6 1.0 copy-done.7
  38.5 1.0 copy-done.9
  39.5 2.8 %collective-permute-done.6.refs_2_ = bf16[48,4096]{1,0:T(8,128)(2,1)} collective-permute-done((bf16[48,4096]{1,0:T(8,128)(2,1)}, bf16[48,4096]{1,0:T(8,128)(2,1)}, u32[]{:S(2)}, u32[]{:S(2)}) %collective-permute-start.6) | collective-permute-done | bytes 393248 | tf_op jit(solution)/shard_map/ppermute | solution.py:50
  42.3 1.7 %collective-permute-done.5.refs_1_ = bf16[48,4096]{1,0:T(8,128)(2,1)} collective-permute-done((bf16[48,4096]{1,0:T(8,128)(2,1)}, bf16[48,4096]{1,0:T(8,128)(2,1)}, u32[]{:S(2)}, u32[]{:S(2)}) %collective-permute-start.5) | collective-permute-done | bytes 393248 | tf_op jit(solution)/shard_map/ppermute | solution.py:50
  44.0 5.4 %all-to-all-done.table_ref = bf16[32,128,128]{2,1,0:T(8,128)(2,1)S(1)} async-done(((bf16[32,128,128]{2,1,0:T(8,128)(2,1)}), bf16[32,128,128]{2,1,0:T(8,128)(2,1)S(1)}, u32[]{:S(2)}, u32[]{:S(2)}) %all-to-all-start) | async-done | bytes 1048608 | tf_op jit(solution)/shard_map/all_to_all | solution.py:474
  49.4 0.6 nearby.1.refs_0_
  50.0 0.0 copy-start.4
  50.0 0.7 collective-permute-start.12
  50.7 3.2 %collective-permute-start.11 = (bf16[12,128,128]{2,1,0:T(8,128)(2,1)S(1)}, bf16[12,128,128]{2,1,0:T(8,128)(2,1)S(1)}, u32[]{:S(2)}, u32[]{:S(2)}) collective-permute-start(bf16[12,128,128]{2,1,0:T(8,128)(2,1)S(1)} %nearby.1.refs_0_), channel_id=1, source_target_pairs={{0,4},{1,5},{2,6},{3,7},{4,0},{5,1},{6,2},{7,3},{8,12},{9,13},{10,... | collective-permute-start | bytes 1179656 | tf_op jit(solution)/shard_map/ppermute | solution.py:50
  53.9 7.8 %gheads.1 = (bf16[192,512]{1,0:T(8,128)(2,1)}, bf16[192,512]{1,0:T(8,128)(2,1)}) custom-call(bf16[48,4096]{1,0:T(8,128)(2,1)} %refs_0_.2, bf16[48,4096]{1,0:T(8,128)(2,1)} %collective-permute-done.5.refs_1_, bf16[48,4096]{1,0:T(8,128)(2,1)} %collective-permute-done.6.refs_2_, bf16[48,4096]{1,0:T(8,128)(2,1)} %collective-permute-done.7.refs_3_, ...), custom_call_target="tpu_custom_call" | custom-call | bytes 1048576 | tf_op jit(solution)/shard_map/gheads/pallas_call | solution.py:126
  61.7 0.1 collective-permute-start.9
  61.8 1.6 %collective-permute-done.9.refs_3_ = bf16[192,512]{1,0:T(8,128)(2,1)S(1)} collective-permute-done((bf16[192,512]{1,0:T(8,128)(2,1)}, bf16[192,512]{1,0:T(8,128)(2,1)S(1)}, u32[]{:S(2)}, u32[]{:S(2)}) %collective-permute-start.9) | collective-permute-done | bytes 196640 | tf_op jit(solution)/shard_map/ppermute | solution.py:54
  63.5 0.9 copy-done.5
  64.4 0.6 assemble.1
  65.0 0.2 collective-permute-start.13
  65.2 3.6 %collective-permute-done.11.refs_2_ = bf16[12,128,128]{2,1,0:T(8,128)(2,1)S(1)} collective-permute-done((bf16[12,128,128]{2,1,0:T(8,128)(2,1)S(1)}, bf16[12,128,128]{2,1,0:T(8,128)(2,1)S(1)}, u32[]{:S(2)}, u32[]{:S(2)}) %collective-permute-start.11) | collective-permute-done | bytes 393248 | tf_op jit(solution)/shard_map/ppermute | solution.py:50
  68.8 0.0 collective-permute-done.10.refs_1_
  68.9 0.5 collective-permute-start.15
  69.4 0.0 collective-permute-start.16
  69.4 1.2 collective-permute-done.14.refs_5_
  70.6 0.6 collective-permute-done.15.refs_6_
  71.1 0.6 collective-permute-done.16.refs_7_
  71.7 12.2 %attend.1 = (bf16[2,192,512]{2,1,0:T(8,128)(2,1)S(1)}, bf16[2,192,512]{2,1,0:T(8,128)(2,1)S(1)}, bf16[4,12,128,128]{3,2,1,0:T(8,128)(2,1)S(1)}, bf16[4,12,128,128]{3,2,1,0:T(8,128)(2,1)S(1)}) custom-call(s32[8]{0:T(128)S(1)} %stack.35.index_ref, bf16[12,128,128]{2,1,0:T(8,128)(2,1)S(1)} %nearby.1.refs_0_, ...), custom_call_target="tpu_custom_call" | custom-call | flops 6442450944 | bytes 1048576 | tf_op jit(solution)/shard_map/attend/pallas_call | solution.py:252
  83.9 0.2 collective-permute-start.17
  84.1 0.4 collective-permute-start.18
  84.5 2.9 %collective-permute-done.17 = bf16[4,12,128,128]{3,2,1,0:T(8,128)(2,1)S(1)} collective-permute-done((bf16[4,12,128,128]{3,2,1,0:T(8,128)(2,1)S(1)}, bf16[4,12,128,128]{3,2,1,0:T(8,128)(2,1)S(1)}, u32[]{:S(2)}, u32[]{:S(2)}) %collective-permute-start.17) | collective-permute-done | bytes 1572896 | tf_op jit(solution)/shard_map/ppermute | solution.py:54
  87.4 0.7 fusion.3
  88.1 2.7 %collective-permute-start.21 = (bf16[12,128,128]{2,1,0:T(8,128)(2,1)S(1)}, bf16[12,128,128]{2,1,0:T(8,128)(2,1)S(1)}, u32[]{:S(2)}, u32[]{:S(2)}) collective-permute-start(bf16[12,128,128]{2,1,0:T(8,128)(2,1)S(1)} %get-tuple-element.79), channel_id=1, source_target_pairs={{0,6},{1,7},{2,0},{3,1},{4,2},{5,3},{6,4},{7,5},{8,14},{9,15},{10,... | collective-permute-start | bytes 1179656 | tf_op jit(solution)/shard_map/ppermute | solution.py:451
  90.8 1.0 collective-permute-start.19
  91.8 8.8 %outs.1 = (bf16[2,48,4096]{2,1,0:T(8,128)(2,1)S(1)}, bf16[2,48,4096]{2,1,0:T(8,128)(2,1)}, bf16[2,48,4096]{2,1,0:T(8,128)(2,1)}, bf16[2,48,4096]{2,1,0:T(8,128)(2,1)S(1)}) custom-call(bf16[2,192,512]{2,1,0:T(8,128)(2,1)S(1)} %get-tuple-element.62.mine_any, bf16[2,192,512]{2,1,0:T(8,128)(2,1)S(1)} %collective-permute-done.18.got_any, ...), custom_call_target="tpu_custom_call" | custom-call | flops 966367616 | bytes 5033164 | tf_op jit(solution)/shard_map/outs/pallas_call | solution.py:305
  100.6 7.4 %collective-permute-done.21.refs_3_ = bf16[12,128,128]{2,1,0:T(8,128)(2,1)S(1)} collective-permute-done((bf16[12,128,128]{2,1,0:T(8,128)(2,1)S(1)}, bf16[12,128,128]{2,1,0:T(8,128)(2,1)S(1)}, u32[]{:S(2)}, u32[]{:S(2)}) %collective-permute-start.21) | collective-permute-done | bytes 393248 | tf_op jit(solution)/shard_map/ppermute | solution.py:451
  107.9 3.4 %collective-permute-done.19.refs_1_ = bf16[12,128,128]{2,1,0:T(8,128)(2,1)S(1)} collective-permute-done((bf16[12,128,128]{2,1,0:T(8,128)(2,1)S(1)}, bf16[12,128,128]{2,1,0:T(8,128)(2,1)S(1)}, u32[]{:S(2)}, u32[]{:S(2)}) %collective-permute-start.19) | collective-permute-done | bytes 393248 | tf_op jit(solution)/shard_map/ppermute | solution.py:451
  111.3 2.4 %collective-permute-start.23 = (bf16[2,48,4096]{2,1,0:T(8,128)(2,1)}, bf16[2,48,4096]{2,1,0:T(8,128)(2,1)}, u32[]{:S(2)}, u32[]{:S(2)}) collective-permute-start(bf16[2,48,4096]{2,1,0:T(8,128)(2,1)} %get-tuple-element.70), channel_id=1, source_target_pairs={{0,4},{1,5},{2,6},{3,7},{4,0},{5,1},{6,2},{7,3},{8,12},{9,13},{10,... | collective-permute-start | bytes 2359304 | tf_op jit(solution)/shard_map/ppermute | solution.py:451
  113.7 0.9 collective-permute-start.24
  114.6 1.7 %place.1 = bf16[32,128,128]{2,1,0:T(8,128)(2,1)} custom-call(s32[12]{0:T(128)S(1)} %bitcast.21, bf16[12,128,128]{2,1,0:T(8,128)(2,1)S(1)} %get-tuple-element.74.refs_0_, bf16[12,128,128]{2,1,0:T(8,128)(2,1)S(1)} %collective-permute-done.19.refs_1_, bf16[12,128,128]{2,1,0:T(8,128)(2,1)S(1)} %collective-permute-done.20.refs_2_, ...), custom_call_target="tpu_custom_call" | custom-call | bytes 4194304 | tf_op jit(solution)/shard_map/place/pallas_call | solution.py:380
  116.3 9.1 %all-to-all-start.1 = ((bf16[32,128,128]{2,1,0:T(8,128)(2,1)}), bf16[32,128,128]{2,1,0:T(8,128)(2,1)S(1)}, u32[]{:S(2)}, u32[]{:S(2)}) async-start(bf16[32,128,128]{2,1,0:T(8,128)(2,1)} %place.1), calls=%async_computation.1 | async-start | bytes 2097152 | tf_op jit(solution)/shard_map/all_to_all | solution.py:496
  125.4 23.4 %collective-permute-done.22.refs_1_ = bf16[2,48,4096]{2,1,0:T(8,128)(2,1)} collective-permute-done((bf16[2,48,4096]{2,1,0:T(8,128)(2,1)}, bf16[2,48,4096]{2,1,0:T(8,128)(2,1)}, u32[]{:S(2)}, u32[]{:S(2)}) %collective-permute-start.22) | collective-permute-done | bytes 786464 | tf_op jit(solution)/shard_map/ppermute | solution.py:451
  148.9 0.6 collective-permute-done.24.refs_3_
  149.5 2.7 %final.1 = (bf16[48,4096]{1,0:T(8,128)(2,1)}, bf16[48,4096]{1,0:T(8,128)(2,1)}) custom-call(bf16[2,48,4096]{2,1,0:T(8,128)(2,1)S(1)} %get-tuple-element.68.refs_0_, bf16[2,48,4096]{2,1,0:T(8,128)(2,1)} %collective-permute-done.22.refs_1_, bf16[2,48,4096]{2,1,0:T(8,128)(2,1)} %collective-permute-done.23.refs_2_, ...), custom_call_target="tpu_custom_call" | custom-call | flops 68719476736 | bytes 4194304 | tf_op jit(solution)/shard_map/final/pallas_call | solution.py:434
  152.2 0.7 all-to-all-done.1.in_ref
  152.9 1.5 collect.1
  (33 shorter events, 0.1 us)
Async XLA Ops:
  0.6 26.1 %collective-permute-start.3 = (bf16[4096,512]{1,0:T(8,128)(2,1)}, bf16[4096,512]{1,0:T(8,128)(2,1)}, u32[]{:S(2)}, u32[]{:S(2)}) collective-permute-start(bf16[4096,512]{1,0:T(8,128)(2,1)} %wq_any.1), channel_id=1, source_target_pairs={{0,1},{1,0},{2,3},{3,2},{4,5},{5,4},{6,7},{7,6},{8,9},{9,8},{10,11... | collective-permute-start | bytes 12582920 | tf_op jit(solution)/shard_map/ppermute | solution.py:54
  0.7 53.2 %collective-permute-start.8 = (bf16[512,4096]{1,0:T(8,128)(2,1)}, bf16[512,4096]{1,0:T(8,128)(2,1)}, u32[]{:S(2)}, u32[]{:S(2)}) collective-permute-start(bf16[512,4096]{1,0:T(8,128)(2,1)} %wo_any.1), channel_id=1, source_target_pairs={{0,1},{1,0},{2,3},{3,2},{4,5},{5,4},{6,7},{7,6},{8,9},{9,8},{10,11... | collective-permute-start | bytes 12582920 | tf_op jit(solution)/shard_map/ppermute | solution.py:54
  1.2 20.7 %collective-permute-start.1 = (bf16[48,4096]{1,0:T(8,128)(2,1)}, bf16[48,4096]{1,0:T(8,128)(2,1)}, u32[]{:S(2)}, u32[]{:S(2)}) collective-permute-start(bf16[48,4096]{1,0:T(8,128)(2,1)} %refs_0_.1), channel_id=1, source_target_pairs={{0,4},{1,5},{2,6},{3,7},{4,0},{5,1},{6,2},{7,3},{8,12},{9,13},{10,... | collective-permute-start | bytes 1179656 | tf_op jit(solution)/shard_map/ppermute | solution.py:50
  4.3 18.5 %collective-permute-start = (bf16[48,4096]{1,0:T(8,128)(2,1)}, bf16[48,4096]{1,0:T(8,128)(2,1)}, u32[]{:S(2)}, u32[]{:S(2)}) collective-permute-start(bf16[48,4096]{1,0:T(8,128)(2,1)} %refs_0_.1), channel_id=1, source_target_pairs={{0,6},{1,7},{2,0},{3,1},{4,2},{5,3},{6,4},{7,5},{8,14},{9,15},{10,... | collective-permute-start | bytes 1179656 | tf_op jit(solution)/shard_map/ppermute | solution.py:50
  5.4 20.4 %collective-permute-start.2 = (bf16[48,4096]{1,0:T(8,128)(2,1)}, bf16[48,4096]{1,0:T(8,128)(2,1)}, u32[]{:S(2)}, u32[]{:S(2)}) collective-permute-start(bf16[48,4096]{1,0:T(8,128)(2,1)} %refs_0_.1), channel_id=1, source_target_pairs={{0,2},{1,3},{2,4},{3,5},{4,6},{5,7},{6,0},{7,1},{8,10},{9,11},{10,... | collective-permute-start | bytes 1179656 | tf_op jit(solution)/shard_map/ppermute | solution.py:50
  10.2 39.2 %all-to-all-start = ((bf16[32,128,128]{2,1,0:T(8,128)(2,1)}), bf16[32,128,128]{2,1,0:T(8,128)(2,1)S(1)}, u32[]{:S(2)}, u32[]{:S(2)}) async-start(bf16[32,128,128]{2,1,0:T(8,128)(2,1)} %outgoing.1), calls=%async_computation | async-start | bytes 2097152 | tf_op jit(solution)/shard_map/all_to_all | solution.py:474
  21.9 11.9 %copy-start.11 = (s32[32,6,2]{0,2,1:T(2,128)S(1)}, s32[32,6,2]{0,2,1:T(2,128)}, u32[]{:S(2)}) copy-start(s32[32,6,2]{0,2,1:T(2,128)} %param.11) | copy-start | bytes 4612
  21.9 12.2 %copy-start.2 = (bf16[1024,512]{1,0:T(8,128)(2,1)S(1)}, bf16[1024,512]{1,0:T(8,128)(2,1)}, u32[]{:S(2)}) copy-start(bf16[1024,512]{1,0:T(8,128)(2,1)} %wk_any) | copy-start | bytes 3145732
  21.9 12.2 %copy-start.3 = (bf16[1024,512]{1,0:T(8,128)(2,1)S(1)}, bf16[1024,512]{1,0:T(8,128)(2,1)}, u32[]{:S(2)}) copy-start(bf16[1024,512]{1,0:T(8,128)(2,1)} %wv_any.1) | copy-start | bytes 3145732
  21.9 17.6 %collective-permute-start.7 = (bf16[48,4096]{1,0:T(8,128)(2,1)}, bf16[48,4096]{1,0:T(8,128)(2,1)}, u32[]{:S(2)}, u32[]{:S(2)}) collective-permute-start(bf16[48,4096]{1,0:T(8,128)(2,1)} %refs_0_.2), channel_id=1, source_target_pairs={{0,2},{1,3},{2,4},{3,5},{4,6},{5,7},{6,0},{7,1},{8,10},{9,11},{10,... | collective-permute-start | bytes 1179656 | tf_op jit(solution)/shard_map/ppermute | solution.py:50
  22.7 19.5 %collective-permute-start.6 = (bf16[48,4096]{1,0:T(8,128)(2,1)}, bf16[48,4096]{1,0:T(8,128)(2,1)}, u32[]{:S(2)}, u32[]{:S(2)}) collective-permute-start(bf16[48,4096]{1,0:T(8,128)(2,1)} %refs_0_.2), channel_id=1, source_target_pairs={{0,4},{1,5},{2,6},{3,7},{4,0},{5,1},{6,2},{7,3},{8,12},{9,13},{10,... | collective-permute-start | bytes 1179656 | tf_op jit(solution)/shard_map/ppermute | solution.py:50
  25.8 18.2 %collective-permute-start.5 = (bf16[48,4096]{1,0:T(8,128)(2,1)}, bf16[48,4096]{1,0:T(8,128)(2,1)}, u32[]{:S(2)}, u32[]{:S(2)}) collective-permute-start(bf16[48,4096]{1,0:T(8,128)(2,1)} %refs_0_.2), channel_id=1, source_target_pairs={{0,6},{1,7},{2,0},{3,1},{4,2},{5,3},{6,4},{7,5},{8,14},{9,15},{10,... | collective-permute-start | bytes 1179656 | tf_op jit(solution)/shard_map/ppermute | solution.py:50
  33.6 15.8 %collective-permute-start.4 = (bf16[192,512]{1,0:T(8,128)(2,1)}, bf16[192,512]{1,0:T(8,128)(2,1)S(1)}, u32[]{:S(2)}, u32[]{:S(2)}) collective-permute-start(bf16[192,512]{1,0:T(8,128)(2,1)} %get-tuple-element.42), channel_id=1, source_target_pairs={{0,1},{1,0},{2,3},{3,2},{4,5},{5,4},{6,7},{7,6},{8,9},{9,8},{10,11... | collective-permute-start | bytes 589832 | tf_op jit(solution)/shard_map/ppermute | solution.py:54
  37.6 1.0 copy-start.7
  38.5 1.0 copy-start.9
  50.0 13.5 %copy-start.4 = (bf16[192,512]{1,0:T(8,128)(2,1)S(1)}, bf16[192,512]{1,0:T(8,128)(2,1)}, u32[]{:S(2)}) copy-start(bf16[192,512]{1,0:T(8,128)(2,1)} %get-tuple-element.41.refs_0_) | copy-start | bytes 589828
  50.0 21.7 %copy-start.8 = (bf16[1024,512]{1,0:T(8,128)(2,1)S(1)}, bf16[1024,512]{1,0:T(8,128)(2,1)}, u32[]{:S(2)}) copy-start(bf16[1024,512]{1,0:T(8,128)(2,1)} %copy-done.7) | copy-start | bytes 3145732
  50.0 21.7 %copy-start.10 = (bf16[1024,512]{1,0:T(8,128)(2,1)S(1)}, bf16[1024,512]{1,0:T(8,128)(2,1)}, u32[]{:S(2)}) copy-start(bf16[1024,512]{1,0:T(8,128)(2,1)} %copy-done.9) | copy-start | bytes 3145732
  50.0 15.2 %collective-permute-start.12 = (bf16[12,128,128]{2,1,0:T(8,128)(2,1)S(1)}, bf16[12,128,128]{2,1,0:T(8,128)(2,1)S(1)}, u32[]{:S(2)}, u32[]{:S(2)}) collective-permute-start(bf16[12,128,128]{2,1,0:T(8,128)(2,1)S(1)} %nearby.1.refs_0_), channel_id=1, source_target_pairs={{0,2},{1,3},{2,4},{3,5},{4,6},{5,7},{6,0},{7,1},{8,10},{9,11},{10,... | collective-permute-start | bytes 1179656 | tf_op jit(solution)/shard_map/ppermute | solution.py:50
  50.7 18.1 %collective-permute-start.11 = (bf16[12,128,128]{2,1,0:T(8,128)(2,1)S(1)}, bf16[12,128,128]{2,1,0:T(8,128)(2,1)S(1)}, u32[]{:S(2)}, u32[]{:S(2)}) collective-permute-start(bf16[12,128,128]{2,1,0:T(8,128)(2,1)S(1)} %nearby.1.refs_0_), channel_id=1, source_target_pairs={{0,4},{1,5},{2,6},{3,7},{4,0},{5,1},{6,2},{7,3},{8,12},{9,13},{10,... | collective-permute-start | bytes 1179656 | tf_op jit(solution)/shard_map/ppermute | solution.py:50
  53.9 15.0 %collective-permute-start.10 = (bf16[12,128,128]{2,1,0:T(8,128)(2,1)S(1)}, bf16[12,128,128]{2,1,0:T(8,128)(2,1)S(1)}, u32[]{:S(2)}, u32[]{:S(2)}) collective-permute-start(bf16[12,128,128]{2,1,0:T(8,128)(2,1)S(1)} %nearby.1.refs_0_), channel_id=1, source_target_pairs={{0,6},{1,7},{2,0},{3,1},{4,2},{5,3},{6,4},{7,5},{8,14},{9,15},{10,... | collective-permute-start | bytes 1179656 | tf_op jit(solution)/shard_map/ppermute | solution.py:50
  61.7 1.7 %collective-permute-start.9 = (bf16[192,512]{1,0:T(8,128)(2,1)}, bf16[192,512]{1,0:T(8,128)(2,1)S(1)}, u32[]{:S(2)}, u32[]{:S(2)}) collective-permute-start(bf16[192,512]{1,0:T(8,128)(2,1)} %get-tuple-element.51), channel_id=1, source_target_pairs={{0,1},{1,0},{2,3},{3,2},{4,5},{5,4},{6,7},{7,6},{8,9},{9,8},{10,11... | collective-permute-start | bytes 589832 | tf_op jit(solution)/shard_map/ppermute | solution.py:54
  63.5 0.9 copy-start.5
  65.0 4.4 %collective-permute-start.13 = (bf16[12,128,128]{2,1,0:T(8,128)(2,1)S(1)}, bf16[12,128,128]{2,1,0:T(8,128)(2,1)S(1)}, u32[]{:S(2)}, u32[]{:S(2)}) collective-permute-start(bf16[12,128,128]{2,1,0:T(8,128)(2,1)S(1)} %nearby.1.refs_0_), channel_id=1, source_target_pairs={{0,1},{1,0},{2,3},{3,2},{4,5},{5,4},{6,7},{7,6},{8,9},{9,8},{10,11... | collective-permute-start | bytes 1179656 | tf_op jit(solution)/shard_map/ppermute | solution.py:54
  68.9 1.7 %collective-permute-start.14 = (bf16[12,128,128]{2,1,0:T(8,128)(2,1)S(1)}, bf16[12,128,128]{2,1,0:T(8,128)(2,1)S(1)}, u32[]{:S(2)}, u32[]{:S(2)}) collective-permute-start(bf16[12,128,128]{2,1,0:T(8,128)(2,1)S(1)} %collective-permute-done.10.refs_1_), channel_id=1, source_target_pairs={{0,1},{1,0},{2,3},{3,2},{4,5},{5,4},{6,7},{7,6},{8,9},{9,8},{10,11... | collective-permute-start | bytes 1179656 | tf_op jit(solution)/shard_map/ppermute | solution.py:54
  68.9 2.3 %collective-permute-start.15 = (bf16[12,128,128]{2,1,0:T(8,128)(2,1)S(1)}, bf16[12,128,128]{2,1,0:T(8,128)(2,1)S(1)}, u32[]{:S(2)}, u32[]{:S(2)}) collective-permute-start(bf16[12,128,128]{2,1,0:T(8,128)(2,1)S(1)} %collective-permute-done.11.refs_2_), channel_id=1, source_target_pairs={{0,1},{1,0},{2,3},{3,2},{4,5},{5,4},{6,7},{7,6},{8,9},{9,8},{10,11... | collective-permute-start | bytes 1179656 | tf_op jit(solution)/shard_map/ppermute | solution.py:54
  69.4 2.3 %collective-permute-start.16 = (bf16[12,128,128]{2,1,0:T(8,128)(2,1)S(1)}, bf16[12,128,128]{2,1,0:T(8,128)(2,1)S(1)}, u32[]{:S(2)}, u32[]{:S(2)}) collective-permute-start(bf16[12,128,128]{2,1,0:T(8,128)(2,1)S(1)} %collective-permute-done.12.refs_3_), channel_id=1, source_target_pairs={{0,1},{1,0},{2,3},{3,2},{4,5},{5,4},{6,7},{7,6},{8,9},{9,8},{10,11... | collective-permute-start | bytes 1179656 | tf_op jit(solution)/shard_map/ppermute | solution.py:54
  71.7 20.1 %copy-start.1 = (bf16[4096,512]{1,0:T(8,128)(2,1)S(1)}, bf16[4096,512]{1,0:T(8,128)(2,1)}, u32[]{:S(2)}) copy-start(bf16[4096,512]{1,0:T(8,128)(2,1)} %wq_any.1) | copy-start | bytes 12582916
  83.9 3.5 %collective-permute-start.17 = (bf16[4,12,128,128]{3,2,1,0:T(8,128)(2,1)S(1)}, bf16[4,12,128,128]{3,2,1,0:T(8,128)(2,1)S(1)}, u32[]{:S(2)}, u32[]{:S(2)}) collective-permute-start(bf16[4,12,128,128]{3,2,1,0:T(8,128)(2,1)S(1)} %get-tuple-element.61), channel_id=1, source_target_pairs={{0,1},{1,0},{2,3},{3,2},{4,5},{5,4},{6,7},{7,6},{8,9},{9,8},{10,11... | collective-permute-start | bytes 4718600 | tf_op jit(solution)/shard_map/ppermute | solution.py:54
  84.1 7.6 %collective-permute-start.18 = (bf16[2,192,512]{2,1,0:T(8,128)(2,1)S(1)}, bf16[2,192,512]{2,1,0:T(8,128)(2,1)S(1)}, u32[]{:S(2)}, u32[]{:S(2)}) collective-permute-start(bf16[2,192,512]{2,1,0:T(8,128)(2,1)S(1)} %get-tuple-element.63), channel_id=1, source_target_pairs={{0,1},{1,0},{2,3},{3,2},{4,5},{5,4},{6,7},{7,6},{8,9},{9,8},{10,11... | collective-permute-start | bytes 1179656 | tf_op jit(solution)/shard_map/ppermute | solution.py:54
  87.4 4.4 %copy-start = (bf16[512,4096]{1,0:T(8,128)(2,1)S(1)}, bf16[512,4096]{1,0:T(8,128)(2,1)}, u32[]{:S(2)}) copy-start(bf16[512,4096]{1,0:T(8,128)(2,1)} %wo_any.1) | copy-start | bytes 12582916
  88.1 19.8 %collective-permute-start.21 = (bf16[12,128,128]{2,1,0:T(8,128)(2,1)S(1)}, bf16[12,128,128]{2,1,0:T(8,128)(2,1)S(1)}, u32[]{:S(2)}, u32[]{:S(2)}) collective-permute-start(bf16[12,128,128]{2,1,0:T(8,128)(2,1)S(1)} %get-tuple-element.79), channel_id=1, source_target_pairs={{0,6},{1,7},{2,0},{3,1},{4,2},{5,3},{6,4},{7,5},{8,14},{9,15},{10,... | collective-permute-start | bytes 1179656 | tf_op jit(solution)/shard_map/ppermute | solution.py:451
  90.8 17.1 %collective-permute-start.20 = (bf16[12,128,128]{2,1,0:T(8,128)(2,1)S(1)}, bf16[12,128,128]{2,1,0:T(8,128)(2,1)S(1)}, u32[]{:S(2)}, u32[]{:S(2)}) collective-permute-start(bf16[12,128,128]{2,1,0:T(8,128)(2,1)S(1)} %get-tuple-element.80), channel_id=1, source_target_pairs={{0,4},{1,5},{2,6},{3,7},{4,0},{5,1},{6,2},{7,3},{8,12},{9,13},{10,... | collective-permute-start | bytes 1179656 | tf_op jit(solution)/shard_map/ppermute | solution.py:451
  90.8 20.5 %collective-permute-start.19 = (bf16[12,128,128]{2,1,0:T(8,128)(2,1)S(1)}, bf16[12,128,128]{2,1,0:T(8,128)(2,1)S(1)}, u32[]{:S(2)}, u32[]{:S(2)}) collective-permute-start(bf16[12,128,128]{2,1,0:T(8,128)(2,1)S(1)} %get-tuple-element.81), channel_id=1, source_target_pairs={{0,2},{1,3},{2,4},{3,5},{4,6},{5,7},{6,0},{7,1},{8,10},{9,11},{10,... | collective-permute-start | bytes 1179656 | tf_op jit(solution)/shard_map/ppermute | solution.py:451
  111.3 37.5 %collective-permute-start.22 = (bf16[2,48,4096]{2,1,0:T(8,128)(2,1)}, bf16[2,48,4096]{2,1,0:T(8,128)(2,1)}, u32[]{:S(2)}, u32[]{:S(2)}) collective-permute-start(bf16[2,48,4096]{2,1,0:T(8,128)(2,1)} %get-tuple-element.69), channel_id=1, source_target_pairs={{0,2},{1,3},{2,4},{3,5},{4,6},{5,7},{6,0},{7,1},{8,10},{9,11},{10,... | collective-permute-start | bytes 2359304 | tf_op jit(solution)/shard_map/ppermute | solution.py:451
  111.3 37.5 %collective-permute-start.23 = (bf16[2,48,4096]{2,1,0:T(8,128)(2,1)}, bf16[2,48,4096]{2,1,0:T(8,128)(2,1)}, u32[]{:S(2)}, u32[]{:S(2)}) collective-permute-start(bf16[2,48,4096]{2,1,0:T(8,128)(2,1)} %get-tuple-element.70), channel_id=1, source_target_pairs={{0,4},{1,5},{2,6},{3,7},{4,0},{5,1},{6,2},{7,3},{8,12},{9,13},{10,... | collective-permute-start | bytes 2359304 | tf_op jit(solution)/shard_map/ppermute | solution.py:451
  113.7 35.8 %collective-permute-start.24 = (bf16[2,48,4096]{2,1,0:T(8,128)(2,1)S(1)}, bf16[2,48,4096]{2,1,0:T(8,128)(2,1)}, u32[]{:S(2)}, u32[]{:S(2)}) collective-permute-start(bf16[2,48,4096]{2,1,0:T(8,128)(2,1)S(1)} %get-tuple-element.71), channel_id=1, source_target_pairs={{0,6},{1,7},{2,0},{3,1},{4,2},{5,3},{6,4},{7,5},{8,14},{9,15},{10,... | collective-permute-start | bytes 2359304 | tf_op jit(solution)/shard_map/ppermute | solution.py:451
  116.3 36.6 %all-to-all-start.1 = ((bf16[32,128,128]{2,1,0:T(8,128)(2,1)}), bf16[32,128,128]{2,1,0:T(8,128)(2,1)S(1)}, u32[]{:S(2)}, u32[]{:S(2)}) async-start(bf16[32,128,128]{2,1,0:T(8,128)(2,1)} %place.1), calls=%async_computation.1 | async-start | bytes 2097152 | tf_op jit(solution)/shard_map/all_to_all | solution.py:496
  125.4 27.5 %copy-start.6 = (s32[32]{0:T(128)S(1)}, s32[32]{0:T(128)}, u32[]{:S(2)}) copy-start(s32[32]{0:T(128)} %select_reduce_fusion.slot_ref) | copy-start | bytes 388

commit v3 on v2

--- a/solution.py
+++ b/solution.py
@@ -125,7 +125,7 @@
     out = jax.ShapeDtypeStruct((length, width), BF)
     return pl.pallas_call(
         functools.partial(project_kernel, cut=cut, transposed=transposed),
-        in_specs=[ANY] * 6,
+        in_specs=[VMEM] * 2 + [ANY] * 4,
         out_specs=[VMEM] * 2,
         scratch_shapes=[
             pltpu.VMEM((length, depth), BF),
@@ -261,14 +261,10 @@
     )(indices, *pieces, q, gh, w_key, w_value)
 
 
-def outs_kernel(mine_any, got_any, wq_any, wqx_any, wo_any, wox_any, *refs, cut):
-    out_refs, (mine_ref, got_ref, wq_ref, wqx_ref, wo_ref, wox_ref, sems) = refs[:XS], refs[XS:]
+def outs_kernel(mine_ref, got_ref, wq_any, wqx_any, wo_any, wox_any, *refs, cut):
+    out_refs, (wq_ref, wqx_ref, wo_ref, wox_ref, sems) = refs[:XS], refs[XS:]
     rows = mine_ref.shape[1] // XS
     steps = wq_ref.shape[0] // cut
-    first = [
-        pltpu.make_async_copy(mine_any, mine_ref, sems.at[4 * steps]),
-        pltpu.make_async_copy(got_any, got_ref, sems.at[4 * steps + 1]),
-    ]
 
     def weights(k):
         part = pl.ds(pl.multiple_of(k * cut, cut), cut)
@@ -276,13 +272,9 @@
         moves += [(w.at[:, part], r.at[:, part]) for w, r in ((wo_any, wo_ref), (wox_any, wox_ref))]
         return [pltpu.make_async_copy(s, d, sems.at[4 * k + i]) for i, (s, d) in enumerate(moves)]
 
-    for copy in first:
-        copy.start()
     for k in range(steps):
         for copy in weights(k):
             copy.start()
-    for copy in first:
-        copy.wait()
 
     def step(k, _):
         for copy in weights(k):
@@ -304,16 +296,14 @@
     cut = full // 8
     return pl.pallas_call(
         functools.partial(outs_kernel, cut=cut),
-        in_specs=[ANY] * 6,
+        in_specs=[VMEM] * 2 + [ANY] * 4,
         out_specs=[VMEM] * XS,
         scratch_shapes=[
-            pltpu.VMEM(mine.shape, BF),
-            pltpu.VMEM(mine.shape, BF),
             pltpu.VMEM(w_query.shape, BF),
             pltpu.VMEM(w_query.shape, BF),
             pltpu.VMEM(w_out.shape, BF),
             pltpu.VMEM(w_out.shape, BF),
-            pltpu.SemaphoreType.DMA((4 * (full // cut) + 2,)),
+            pltpu.SemaphoreType.DMA((4 * (full // cut),)),
         ],
         out_shape=[jax.ShapeDtypeStruct((2, length // XS, full), BF)] * XS,
         compiler_params=params(B_OUTS),
@@ -361,7 +351,7 @@
         out_specs=VMEM,
         scratch_shapes=[pltpu.VMEM((count, depth, cols), BF), pltpu.SemaphoreType.DMA(())],
         out_shape=jax.ShapeDtypeStruct((slot.shape[0], depth, cols), BF),
-        compiler_params=params(BIG),
+        compiler_params=params(16),
         cost_estimate=cost(0, 1 << 20),
         name="outgoing",
     )(slot, at, table)

time: 155 us -> 155 us (level)
  waiting for transfers between devices: 56 us -> 53.9 us
    pallas_call x2, Pallas kernels: 14.7 us -> 17.2 us  [project(): pl.pallas_call(functools.partial(project_kernel, cut=cut, transposed=tran...]
    ppermute x9, waiting for transfers between devices: 8.26 us -> 6.07 us  [x_pieces(): lax.ppermute(block, 'mp', x_perm(-i))]
where the time goes in v3:
time: 155 us
  waiting for transfers between devices  53.9 us (35%)
  Pallas kernels  50.1 us (32%)
  starting transfers between devices  43.8 us (28%)
  local copies, waits for them, and re-layouts  4.39 us (3%)
    ppermute x6, waiting for transfers between devices, x_parts(): lax.ppermute(sums[i], 'mp', x_perm(i))  34.9 us
    pallas_call x2, Pallas kernels, project(): pl.pallas_call(functools.partial(project_kernel, cut=cut, transposed=tran...  17.2 us
    ppermute x9, starting transfers between devices, x_pieces(): lax.ppermute(block, 'mp', x_perm(-i))  13.6 us
    pallas_call x1, Pallas kernels, attend(): pl.pallas_call(attend_kernel, in_specs=[SMEM] + [VMEM] * 12, out_specs=[V...  12.2 us
    all_to_all x1, starting transfers between devices, body(): lax.all_to_all(outgoing, 'dp', split_axis=0, concat_axis=0, tiled=True)  11.7 us
    all_to_all x1, starting transfers between devices, body(): lax.all_to_all(place_sums(my_owners, parts[0], dp_count), 'dp', split_axi...  9.4 us
    pallas_call x1, Pallas kernels, outs(): pl.pallas_call(functools.partial(outs_kernel, cut=cut), in_specs=[VMEM] *...  8.38 us
    ppermute x6, starting transfers between devices, x_parts(): lax.ppermute(sums[i], 'mp', x_perm(i))  6.91 us
  transfers between devices with their start and end apart: 27, of which 15 were waited for; matrix products, arithmetic and copies ran while one was open for 1% of the time, Pallas kernels for 23%

profile of v3, /device:TPU:8, one launch (start us, length us, event | category | flops | bytes accessed | tf_op | source)
XLA Modules:
  0.0 154.6 jit_solution(13698716721332029334)
XLA Ops:
  0.6 0.1 collective-permute-start.3
  0.7 0.5 collective-permute-start.8
  1.2 3.0 %collective-permute-start.1 = (bf16[48,4096]{1,0:T(8,128)(2,1)}, bf16[48,4096]{1,0:T(8,128)(2,1)}, u32[]{:S(2)}, u32[]{:S(2)}) collective-permute-start(bf16[48,4096]{1,0:T(8,128)(2,1)} %refs_0_.1), channel_id=1, source_target_pairs={{0,4},{1,5},{2,6},{3,7},{4,0},{5,1},{6,2},{7,3},{8,12},{9,13},{10,... | collective-permute-start | bytes 1179656 | tf_op jit(solution)/shard_map/ppermute | solution.py:50
  4.3 1.1 collective-permute-start
  5.4 0.9 collective-permute-start.2
  6.3 0.7 select_reduce_fusion.slot_ref
  7.0 1.2 copy-done.4
  8.2 1.6 %outgoing.1 = bf16[32,128,128]{2,1,0:T(8,128)(2,1)} custom-call(s32[32]{0:T(128)S(1)} %select_reduce_fusion.slot_ref, s32[1]{0:T(128)} %bitcast.9.at_ref, bf16[4,128,1024]{2,1,0:T(8,128)(2,1)S(1)} %copy-done.4), custom_call_target="tpu_custom_call" | custom-call | bytes 1048576 | tf_op jit(solution)/shard_map/outgoing/pallas_call | solution.py:348
  9.9 11.7 %all-to-all-start = ((bf16[32,128,128]{2,1,0:T(8,128)(2,1)}), bf16[32,128,128]{2,1,0:T(8,128)(2,1)S(1)}, u32[]{:S(2)}, u32[]{:S(2)}) async-start(bf16[32,128,128]{2,1,0:T(8,128)(2,1)} %outgoing.1), calls=%async_computation | async-start | bytes 2097152 | tf_op jit(solution)/shard_map/all_to_all | solution.py:464
  21.6 0.0 copy-start.11
  21.6 0.0 copy-start.2
  21.6 0.0 copy-start.3
  21.6 0.7 collective-permute-start.7
  22.3 0.4 collective-permute-done.refs_1_
  22.7 2.8 %collective-permute-start.6 = (bf16[48,4096]{1,0:T(8,128)(2,1)}, bf16[48,4096]{1,0:T(8,128)(2,1)}, u32[]{:S(2)}, u32[]{:S(2)}) collective-permute-start(bf16[48,4096]{1,0:T(8,128)(2,1)} %refs_0_.2), channel_id=1, source_target_pairs={{0,4},{1,5},{2,6},{3,7},{4,0},{5,1},{6,2},{7,3},{8,12},{9,13},{10,... | collective-permute-start | bytes 1179656 | tf_op jit(solution)/shard_map/ppermute | solution.py:50
  25.5 0.0 collective-permute-done.2.refs_3_
  25.5 1.2 collective-permute-start.5
  26.8 8.1 %query.1 = (bf16[192,512]{1,0:T(8,128)(2,1)}, bf16[192,512]{1,0:T(8,128)(2,1)}) custom-call(bf16[48,4096]{1,0:T(8,128)(2,1)} %refs_0_.1, bf16[48,4096]{1,0:T(8,128)(2,1)} %collective-permute-done.refs_1_, bf16[48,4096]{1,0:T(8,128)(2,1)} %collective-permute-done.1.refs_2_, bf16[48,4096]{1,0:T(8,128)(2,1)} %collective-permute-done.2.refs_3_, ...), custom_call_target="tpu_custom_call" | custom-call | flops 25769803776 | bytes 1048576 | tf_op jit(solution)/shard_map/query/pallas_call | solution.py:126
  34.9 0.1 collective-permute-start.4
  35.1 0.1 constant_dynamic-slice_fusion
  35.2 0.1 copy.13
  35.3 0.1 stack.35.index_ref
  35.4 3.4 %arrange.1 = (bf16[1024,512]{1,0:T(8,128)(2,1)S(1)}, bf16[1024,512]{1,0:T(8,128)(2,1)S(1)}) custom-call(s32[8]{0:T(128)S(1)} %stack.35.index_ref, bf16[1024,512]{1,0:T(8,128)(2,1)S(1)} %copy-done.2, bf16[1024,512]{1,0:T(8,128)(2,1)S(1)} %copy-done.3), custom_call_target="tpu_custom_call" | custom-call | bytes 1048576 | tf_op jit(solution)/shard_map/arrange/pallas_call | solution.py:160
  38.8 1.0 copy-done.7
  39.8 1.0 copy-done.9
  40.8 1.2 collective-permute-done.6.refs_2_
  42.0 2.0 %collective-permute-done.5.refs_1_ = bf16[48,4096]{1,0:T(8,128)(2,1)} collective-permute-done((bf16[48,4096]{1,0:T(8,128)(2,1)}, bf16[48,4096]{1,0:T(8,128)(2,1)}, u32[]{:S(2)}, u32[]{:S(2)}) %collective-permute-start.5) | collective-permute-done | bytes 393248 | tf_op jit(solution)/shard_map/ppermute | solution.py:50
  44.0 5.1 %all-to-all-done.table_ref = bf16[32,128,128]{2,1,0:T(8,128)(2,1)S(1)} async-done(((bf16[32,128,128]{2,1,0:T(8,128)(2,1)}), bf16[32,128,128]{2,1,0:T(8,128)(2,1)S(1)}, u32[]{:S(2)}, u32[]{:S(2)}) %all-to-all-start) | async-done | bytes 1048608 | tf_op jit(solution)/shard_map/all_to_all | solution.py:464
  49.1 0.6 nearby.1.refs_0_
  49.7 0.0 copy-start.5
  49.7 0.7 collective-permute-start.12
  50.4 3.2 %collective-permute-start.11 = (bf16[12,128,128]{2,1,0:T(8,128)(2,1)S(1)}, bf16[12,128,128]{2,1,0:T(8,128)(2,1)S(1)}, u32[]{:S(2)}, u32[]{:S(2)}) collective-permute-start(bf16[12,128,128]{2,1,0:T(8,128)(2,1)S(1)} %nearby.1.refs_0_), channel_id=1, source_target_pairs={{0,4},{1,5},{2,6},{3,7},{4,0},{5,1},{6,2},{7,3},{8,12},{9,13},{10,... | collective-permute-start | bytes 1179656 | tf_op jit(solution)/shard_map/ppermute | solution.py:50
  53.6 9.1 %gheads.1 = (bf16[192,512]{1,0:T(8,128)(2,1)}, bf16[192,512]{1,0:T(8,128)(2,1)}) custom-call(bf16[48,4096]{1,0:T(8,128)(2,1)} %refs_0_.2, bf16[48,4096]{1,0:T(8,128)(2,1)} %collective-permute-done.5.refs_1_, bf16[48,4096]{1,0:T(8,128)(2,1)} %collective-permute-done.6.refs_2_, bf16[48,4096]{1,0:T(8,128)(2,1)} %collective-permute-done.7.refs_3_, ...), custom_call_target="tpu_custom_call" | custom-call | bytes 1048576 | tf_op jit(solution)/shard_map/gheads/pallas_call | solution.py:126
  62.7 0.1 collective-permute-start.9
  62.8 1.6 %collective-permute-done.9.refs_3_ = bf16[192,512]{1,0:T(8,128)(2,1)S(1)} collective-permute-done((bf16[192,512]{1,0:T(8,128)(2,1)}, bf16[192,512]{1,0:T(8,128)(2,1)S(1)}, u32[]{:S(2)}, u32[]{:S(2)}) %collective-permute-start.9) | collective-permute-done | bytes 196640 | tf_op jit(solution)/shard_map/ppermute | solution.py:54
  64.4 0.9 copy-done.6
  65.3 0.6 assemble.1
  65.9 0.2 collective-permute-start.13
  66.2 2.3 %collective-permute-done.11.refs_2_ = bf16[12,128,128]{2,1,0:T(8,128)(2,1)S(1)} collective-permute-done((bf16[12,128,128]{2,1,0:T(8,128)(2,1)S(1)}, bf16[12,128,128]{2,1,0:T(8,128)(2,1)S(1)}, u32[]{:S(2)}, u32[]{:S(2)}) %collective-permute-start.11) | collective-permute-done | bytes 393248 | tf_op jit(solution)/shard_map/ppermute | solution.py:50
  68.5 0.0 collective-permute-done.10.refs_1_
  68.6 0.5 collective-permute-start.15
  69.1 0.0 collective-permute-start.16
  69.1 1.2 collective-permute-done.14.refs_5_
  70.3 0.6 collective-permute-done.15.refs_6_
  70.8 0.6 collective-permute-done.16.refs_7_
  71.4 12.2 %attend.1 = (bf16[2,192,512]{2,1,0:T(8,128)(2,1)S(1)}, bf16[2,192,512]{2,1,0:T(8,128)(2,1)S(1)}, bf16[4,12,128,128]{3,2,1,0:T(8,128)(2,1)S(1)}, bf16[4,12,128,128]{3,2,1,0:T(8,128)(2,1)S(1)}) custom-call(s32[8]{0:T(128)S(1)} %stack.35.index_ref, bf16[12,128,128]{2,1,0:T(8,128)(2,1)S(1)} %nearby.1.refs_0_, ...), custom_call_target="tpu_custom_call" | custom-call | flops 6442450944 | bytes 1048576 | tf_op jit(solution)/shard_map/attend/pallas_call | solution.py:252
  83.6 0.2 collective-permute-start.17
  83.8 0.4 collective-permute-start.18
  84.2 2.9 %collective-permute-done.17 = bf16[4,12,128,128]{3,2,1,0:T(8,128)(2,1)S(1)} collective-permute-done((bf16[4,12,128,128]{3,2,1,0:T(8,128)(2,1)S(1)}, bf16[4,12,128,128]{3,2,1,0:T(8,128)(2,1)S(1)}, u32[]{:S(2)}, u32[]{:S(2)}) %collective-permute-start.17) | collective-permute-done | bytes 1572896 | tf_op jit(solution)/shard_map/ppermute | solution.py:54
  87.1 0.7 fusion.3
  87.8 2.7 %collective-permute-start.21 = (bf16[12,128,128]{2,1,0:T(8,128)(2,1)S(1)}, bf16[12,128,128]{2,1,0:T(8,128)(2,1)S(1)}, u32[]{:S(2)}, u32[]{:S(2)}) collective-permute-start(bf16[12,128,128]{2,1,0:T(8,128)(2,1)S(1)} %get-tuple-element.79), channel_id=1, source_target_pairs={{0,6},{1,7},{2,0},{3,1},{4,2},{5,3},{6,4},{7,5},{8,14},{9,15},{10,... | collective-permute-start | bytes 1179656 | tf_op jit(solution)/shard_map/ppermute | solution.py:441
  90.5 1.0 collective-permute-start.19
  91.5 8.4 %outs.1 = (bf16[2,48,4096]{2,1,0:T(8,128)(2,1)S(1)}, bf16[2,48,4096]{2,1,0:T(8,128)(2,1)}, bf16[2,48,4096]{2,1,0:T(8,128)(2,1)}, bf16[2,48,4096]{2,1,0:T(8,128)(2,1)S(1)}) custom-call(bf16[2,192,512]{2,1,0:T(8,128)(2,1)S(1)} %get-tuple-element.62.mine_ref, bf16[2,192,512]{2,1,0:T(8,128)(2,1)S(1)} %collective-permute-done.18.got_ref, ...), custom_call_target="tpu_custom_call" | custom-call | flops 966367616 | bytes 5033164 | tf_op jit(solution)/shard_map/outs/pallas_call | solution.py:297
  99.9 7.8 %collective-permute-done.21.refs_3_ = bf16[12,128,128]{2,1,0:T(8,128)(2,1)S(1)} collective-permute-done((bf16[12,128,128]{2,1,0:T(8,128)(2,1)S(1)}, bf16[12,128,128]{2,1,0:T(8,128)(2,1)S(1)}, u32[]{:S(2)}, u32[]{:S(2)}) %collective-permute-start.21) | collective-permute-done | bytes 393248 | tf_op jit(solution)/shard_map/ppermute | solution.py:441
  107.6 3.4 %collective-permute-done.19.refs_1_ = bf16[12,128,128]{2,1,0:T(8,128)(2,1)S(1)} collective-permute-done((bf16[12,128,128]{2,1,0:T(8,128)(2,1)S(1)}, bf16[12,128,128]{2,1,0:T(8,128)(2,1)S(1)}, u32[]{:S(2)}, u32[]{:S(2)}) %collective-permute-start.19) | collective-permute-done | bytes 393248 | tf_op jit(solution)/shard_map/ppermute | solution.py:441
  111.0 2.4 %collective-permute-start.23 = (bf16[2,48,4096]{2,1,0:T(8,128)(2,1)}, bf16[2,48,4096]{2,1,0:T(8,128)(2,1)}, u32[]{:S(2)}, u32[]{:S(2)}) collective-permute-start(bf16[2,48,4096]{2,1,0:T(8,128)(2,1)} %get-tuple-element.70), channel_id=1, source_target_pairs={{0,4},{1,5},{2,6},{3,7},{4,0},{5,1},{6,2},{7,3},{8,12},{9,13},{10,... | collective-permute-start | bytes 2359304 | tf_op jit(solution)/shard_map/ppermute | solution.py:441
  113.4 0.9 collective-permute-start.24
  114.3 1.7 %place.1 = bf16[32,128,128]{2,1,0:T(8,128)(2,1)} custom-call(s32[12]{0:T(128)S(1)} %bitcast.21, bf16[12,128,128]{2,1,0:T(8,128)(2,1)S(1)} %get-tuple-element.74.refs_0_, bf16[12,128,128]{2,1,0:T(8,128)(2,1)S(1)} %collective-permute-done.19.refs_1_, bf16[12,128,128]{2,1,0:T(8,128)(2,1)S(1)} %collective-permute-done.20.refs_2_, ...), custom_call_target="tpu_custom_call" | custom-call | bytes 4194304 | tf_op jit(solution)/shard_map/place/pallas_call | solution.py:370
  116.0 9.4 %all-to-all-start.1 = ((bf16[32,128,128]{2,1,0:T(8,128)(2,1)}), bf16[32,128,128]{2,1,0:T(8,128)(2,1)S(1)}, u32[]{:S(2)}, u32[]{:S(2)}) async-start(bf16[32,128,128]{2,1,0:T(8,128)(2,1)} %place.1), calls=%async_computation.1 | async-start | bytes 2097152 | tf_op jit(solution)/shard_map/all_to_all | solution.py:486
  125.4 23.1 %collective-permute-done.22.refs_1_ = bf16[2,48,4096]{2,1,0:T(8,128)(2,1)} collective-permute-done((bf16[2,48,4096]{2,1,0:T(8,128)(2,1)}, bf16[2,48,4096]{2,1,0:T(8,128)(2,1)}, u32[]{:S(2)}, u32[]{:S(2)}) %collective-permute-start.22) | collective-permute-done | bytes 786464 | tf_op jit(solution)/shard_map/ppermute | solution.py:441
  148.6 0.6 collective-permute-done.24.refs_3_
  149.2 2.7 %final.1 = (bf16[48,4096]{1,0:T(8,128)(2,1)}, bf16[48,4096]{1,0:T(8,128)(2,1)}) custom-call(bf16[2,48,4096]{2,1,0:T(8,128)(2,1)S(1)} %get-tuple-element.68.refs_0_, bf16[2,48,4096]{2,1,0:T(8,128)(2,1)} %collective-permute-done.22.refs_1_, bf16[2,48,4096]{2,1,0:T(8,128)(2,1)} %collective-permute-done.23.refs_2_, ...), custom_call_target="tpu_custom_call" | custom-call | flops 68719476736 | bytes 4194304 | tf_op jit(solution)/shard_map/final/pallas_call | solution.py:424
  151.9 1.0 all-to-all-done.1.in_ref
  152.9 1.7 %collect.1 = f32[4,128,128]{2,1,0:T(8,128)} custom-call(s32[32]{0:T(128)S(1)} %select_reduce_fusion.slot_ref, s32[32]{0:T(128)S(1)} %convert_element_type.75.held_ref, bf16[32,128,128]{2,1,0:T(8,128)(2,1)S(1)} %all-to-all-done.1.in_ref), custom_call_target="tpu_custom_call" | custom-call | bytes 2097152 | tf_op jit(solution)/shard_map/collect/pallas_call | solution.py:392
  (33 shorter events, 0.1 us)
Async XLA Ops:
  0.6 26.1 %collective-permute-start.3 = (bf16[4096,512]{1,0:T(8,128)(2,1)}, bf16[4096,512]{1,0:T(8,128)(2,1)}, u32[]{:S(2)}, u32[]{:S(2)}) collective-permute-start(bf16[4096,512]{1,0:T(8,128)(2,1)} %wq_any.1), channel_id=1, source_target_pairs={{0,1},{1,0},{2,3},{3,2},{4,5},{5,4},{6,7},{7,6},{8,9},{9,8},{10,11... | collective-permute-start | bytes 12582920 | tf_op jit(solution)/shard_map/ppermute | solution.py:54
  0.7 52.9 %collective-permute-start.8 = (bf16[512,4096]{1,0:T(8,128)(2,1)}, bf16[512,4096]{1,0:T(8,128)(2,1)}, u32[]{:S(2)}, u32[]{:S(2)}) collective-permute-start(bf16[512,4096]{1,0:T(8,128)(2,1)} %wo_any.1), channel_id=1, source_target_pairs={{0,1},{1,0},{2,3},{3,2},{4,5},{5,4},{6,7},{7,6},{8,9},{9,8},{10,11... | collective-permute-start | bytes 12582920 | tf_op jit(solution)/shard_map/ppermute | solution.py:54
  1.2 20.4 %collective-permute-start.1 = (bf16[48,4096]{1,0:T(8,128)(2,1)}, bf16[48,4096]{1,0:T(8,128)(2,1)}, u32[]{:S(2)}, u32[]{:S(2)}) collective-permute-start(bf16[48,4096]{1,0:T(8,128)(2,1)} %refs_0_.1), channel_id=1, source_target_pairs={{0,4},{1,5},{2,6},{3,7},{4,0},{5,1},{6,2},{7,3},{8,12},{9,13},{10,... | collective-permute-start | bytes 1179656 | tf_op jit(solution)/shard_map/ppermute | solution.py:50
  4.3 18.5 %collective-permute-start = (bf16[48,4096]{1,0:T(8,128)(2,1)}, bf16[48,4096]{1,0:T(8,128)(2,1)}, u32[]{:S(2)}, u32[]{:S(2)}) collective-permute-start(bf16[48,4096]{1,0:T(8,128)(2,1)} %refs_0_.1), channel_id=1, source_target_pairs={{0,6},{1,7},{2,0},{3,1},{4,2},{5,3},{6,4},{7,5},{8,14},{9,15},{10,... | collective-permute-start | bytes 1179656 | tf_op jit(solution)/shard_map/ppermute | solution.py:50
  5.4 20.1 %collective-permute-start.2 = (bf16[48,4096]{1,0:T(8,128)(2,1)}, bf16[48,4096]{1,0:T(8,128)(2,1)}, u32[]{:S(2)}, u32[]{:S(2)}) collective-permute-start(bf16[48,4096]{1,0:T(8,128)(2,1)} %refs_0_.1), channel_id=1, source_target_pairs={{0,2},{1,3},{2,4},{3,5},{4,6},{5,7},{6,0},{7,1},{8,10},{9,11},{10,... | collective-permute-start | bytes 1179656 | tf_op jit(solution)/shard_map/ppermute | solution.py:50
  7.0 1.2 copy-start.4
  9.9 39.2 %all-to-all-start = ((bf16[32,128,128]{2,1,0:T(8,128)(2,1)}), bf16[32,128,128]{2,1,0:T(8,128)(2,1)S(1)}, u32[]{:S(2)}, u32[]{:S(2)}) async-start(bf16[32,128,128]{2,1,0:T(8,128)(2,1)} %outgoing.1), calls=%async_computation | async-start | bytes 2097152 | tf_op jit(solution)/shard_map/all_to_all | solution.py:464
  21.6 13.5 %copy-start.11 = (s32[32,6,2]{0,2,1:T(2,128)S(1)}, s32[32,6,2]{0,2,1:T(2,128)}, u32[]{:S(2)}) copy-start(s32[32,6,2]{0,2,1:T(2,128)} %param.11) | copy-start | bytes 4612
  21.6 13.7 %copy-start.2 = (bf16[1024,512]{1,0:T(8,128)(2,1)S(1)}, bf16[1024,512]{1,0:T(8,128)(2,1)}, u32[]{:S(2)}) copy-start(bf16[1024,512]{1,0:T(8,128)(2,1)} %wk_any) | copy-start | bytes 3145732
  21.6 13.7 %copy-start.3 = (bf16[1024,512]{1,0:T(8,128)(2,1)S(1)}, bf16[1024,512]{1,0:T(8,128)(2,1)}, u32[]{:S(2)}) copy-start(bf16[1024,512]{1,0:T(8,128)(2,1)} %wv_any.1) | copy-start | bytes 3145732
  21.6 19.1 %collective-permute-start.7 = (bf16[48,4096]{1,0:T(8,128)(2,1)}, bf16[48,4096]{1,0:T(8,128)(2,1)}, u32[]{:S(2)}, u32[]{:S(2)}) collective-permute-start(bf16[48,4096]{1,0:T(8,128)(2,1)} %refs_0_.2), channel_id=1, source_target_pairs={{0,2},{1,3},{2,4},{3,5},{4,6},{5,7},{6,0},{7,1},{8,10},{9,11},{10,... | collective-permute-start | bytes 1179656 | tf_op jit(solution)/shard_map/ppermute | solution.py:50
  22.7 19.2 %collective-permute-start.6 = (bf16[48,4096]{1,0:T(8,128)(2,1)}, bf16[48,4096]{1,0:T(8,128)(2,1)}, u32[]{:S(2)}, u32[]{:S(2)}) collective-permute-start(bf16[48,4096]{1,0:T(8,128)(2,1)} %refs_0_.2), channel_id=1, source_target_pairs={{0,4},{1,5},{2,6},{3,7},{4,0},{5,1},{6,2},{7,3},{8,12},{9,13},{10,... | collective-permute-start | bytes 1179656 | tf_op jit(solution)/shard_map/ppermute | solution.py:50
  25.5 18.5 %collective-permute-start.5 = (bf16[48,4096]{1,0:T(8,128)(2,1)}, bf16[48,4096]{1,0:T(8,128)(2,1)}, u32[]{:S(2)}, u32[]{:S(2)}) collective-permute-start(bf16[48,4096]{1,0:T(8,128)(2,1)} %refs_0_.2), channel_id=1, source_target_pairs={{0,6},{1,7},{2,0},{3,1},{4,2},{5,3},{6,4},{7,5},{8,14},{9,15},{10,... | collective-permute-start | bytes 1179656 | tf_op jit(solution)/shard_map/ppermute | solution.py:50
  34.9 14.2 %collective-permute-start.4 = (bf16[192,512]{1,0:T(8,128)(2,1)}, bf16[192,512]{1,0:T(8,128)(2,1)S(1)}, u32[]{:S(2)}, u32[]{:S(2)}) collective-permute-start(bf16[192,512]{1,0:T(8,128)(2,1)} %get-tuple-element.42), channel_id=1, source_target_pairs={{0,1},{1,0},{2,3},{3,2},{4,5},{5,4},{6,7},{7,6},{8,9},{9,8},{10,11... | collective-permute-start | bytes 589832 | tf_op jit(solution)/shard_map/ppermute | solution.py:54
  38.8 1.0 copy-start.7
  39.8 1.0 copy-start.9
  49.7 14.7 %copy-start.5 = (bf16[192,512]{1,0:T(8,128)(2,1)S(1)}, bf16[192,512]{1,0:T(8,128)(2,1)}, u32[]{:S(2)}) copy-start(bf16[192,512]{1,0:T(8,128)(2,1)} %get-tuple-element.41.refs_0_) | copy-start | bytes 589828
  49.7 21.7 %copy-start.8 = (bf16[1024,512]{1,0:T(8,128)(2,1)S(1)}, bf16[1024,512]{1,0:T(8,128)(2,1)}, u32[]{:S(2)}) copy-start(bf16[1024,512]{1,0:T(8,128)(2,1)} %copy-done.7) | copy-start | bytes 3145732
  49.7 21.7 %copy-start.10 = (bf16[1024,512]{1,0:T(8,128)(2,1)S(1)}, bf16[1024,512]{1,0:T(8,128)(2,1)}, u32[]{:S(2)}) copy-start(bf16[1024,512]{1,0:T(8,128)(2,1)} %copy-done.9) | copy-start | bytes 3145732
  49.7 16.5 %collective-permute-start.12 = (bf16[12,128,128]{2,1,0:T(8,128)(2,1)S(1)}, bf16[12,128,128]{2,1,0:T(8,128)(2,1)S(1)}, u32[]{:S(2)}, u32[]{:S(2)}) collective-permute-start(bf16[12,128,128]{2,1,0:T(8,128)(2,1)S(1)} %nearby.1.refs_0_), channel_id=1, source_target_pairs={{0,2},{1,3},{2,4},{3,5},{4,6},{5,7},{6,0},{7,1},{8,10},{9,11},{10,... | collective-permute-start | bytes 1179656 | tf_op jit(solution)/shard_map/ppermute | solution.py:50
  50.4 18.1 %collective-permute-start.11 = (bf16[12,128,128]{2,1,0:T(8,128)(2,1)S(1)}, bf16[12,128,128]{2,1,0:T(8,128)(2,1)S(1)}, u32[]{:S(2)}, u32[]{:S(2)}) collective-permute-start(bf16[12,128,128]{2,1,0:T(8,128)(2,1)S(1)} %nearby.1.refs_0_), channel_id=1, source_target_pairs={{0,4},{1,5},{2,6},{3,7},{4,0},{5,1},{6,2},{7,3},{8,12},{9,13},{10,... | collective-permute-start | bytes 1179656 | tf_op jit(solution)/shard_map/ppermute | solution.py:50
  53.6 15.0 %collective-permute-start.10 = (bf16[12,128,128]{2,1,0:T(8,128)(2,1)S(1)}, bf16[12,128,128]{2,1,0:T(8,128)(2,1)S(1)}, u32[]{:S(2)}, u32[]{:S(2)}) collective-permute-start(bf16[12,128,128]{2,1,0:T(8,128)(2,1)S(1)} %nearby.1.refs_0_), channel_id=1, source_target_pairs={{0,6},{1,7},{2,0},{3,1},{4,2},{5,3},{6,4},{7,5},{8,14},{9,15},{10,... | collective-permute-start | bytes 1179656 | tf_op jit(solution)/shard_map/ppermute | solution.py:50
  62.7 1.7 %collective-permute-start.9 = (bf16[192,512]{1,0:T(8,128)(2,1)}, bf16[192,512]{1,0:T(8,128)(2,1)S(1)}, u32[]{:S(2)}, u32[]{:S(2)}) collective-permute-start(bf16[192,512]{1,0:T(8,128)(2,1)} %get-tuple-element.51), channel_id=1, source_target_pairs={{0,1},{1,0},{2,3},{3,2},{4,5},{5,4},{6,7},{7,6},{8,9},{9,8},{10,11... | collective-permute-start | bytes 589832 | tf_op jit(solution)/shard_map/ppermute | solution.py:54
  64.4 0.9 copy-start.6
  65.9 3.1 %collective-permute-start.13 = (bf16[12,128,128]{2,1,0:T(8,128)(2,1)S(1)}, bf16[12,128,128]{2,1,0:T(8,128)(2,1)S(1)}, u32[]{:S(2)}, u32[]{:S(2)}) collective-permute-start(bf16[12,128,128]{2,1,0:T(8,128)(2,1)S(1)} %nearby.1.refs_0_), channel_id=1, source_target_pairs={{0,1},{1,0},{2,3},{3,2},{4,5},{5,4},{6,7},{7,6},{8,9},{9,8},{10,11... | collective-permute-start | bytes 1179656 | tf_op jit(solution)/shard_map/ppermute | solution.py:54
  68.6 1.7 %collective-permute-start.14 = (bf16[12,128,128]{2,1,0:T(8,128)(2,1)S(1)}, bf16[12,128,128]{2,1,0:T(8,128)(2,1)S(1)}, u32[]{:S(2)}, u32[]{:S(2)}) collective-permute-start(bf16[12,128,128]{2,1,0:T(8,128)(2,1)S(1)} %collective-permute-done.10.refs_1_), channel_id=1, source_target_pairs={{0,1},{1,0},{2,3},{3,2},{4,5},{5,4},{6,7},{7,6},{8,9},{9,8},{10,11... | collective-permute-start | bytes 1179656 | tf_op jit(solution)/shard_map/ppermute | solution.py:54
  68.6 2.3 %collective-permute-start.15 = (bf16[12,128,128]{2,1,0:T(8,128)(2,1)S(1)}, bf16[12,128,128]{2,1,0:T(8,128)(2,1)S(1)}, u32[]{:S(2)}, u32[]{:S(2)}) collective-permute-start(bf16[12,128,128]{2,1,0:T(8,128)(2,1)S(1)} %collective-permute-done.11.refs_2_), channel_id=1, source_target_pairs={{0,1},{1,0},{2,3},{3,2},{4,5},{5,4},{6,7},{7,6},{8,9},{9,8},{10,11... | collective-permute-start | bytes 1179656 | tf_op jit(solution)/shard_map/ppermute | solution.py:54
  69.1 2.3 %collective-permute-start.16 = (bf16[12,128,128]{2,1,0:T(8,128)(2,1)S(1)}, bf16[12,128,128]{2,1,0:T(8,128)(2,1)S(1)}, u32[]{:S(2)}, u32[]{:S(2)}) collective-permute-start(bf16[12,128,128]{2,1,0:T(8,128)(2,1)S(1)} %collective-permute-done.12.refs_3_), channel_id=1, source_target_pairs={{0,1},{1,0},{2,3},{3,2},{4,5},{5,4},{6,7},{7,6},{8,9},{9,8},{10,11... | collective-permute-start | bytes 1179656 | tf_op jit(solution)/shard_map/ppermute | solution.py:54
  71.4 20.1 %copy-start.1 = (bf16[4096,512]{1,0:T(8,128)(2,1)S(1)}, bf16[4096,512]{1,0:T(8,128)(2,1)}, u32[]{:S(2)}) copy-start(bf16[4096,512]{1,0:T(8,128)(2,1)} %wq_any.1) | copy-start | bytes 12582916
  83.6 3.5 %collective-permute-start.17 = (bf16[4,12,128,128]{3,2,1,0:T(8,128)(2,1)S(1)}, bf16[4,12,128,128]{3,2,1,0:T(8,128)(2,1)S(1)}, u32[]{:S(2)}, u32[]{:S(2)}) collective-permute-start(bf16[4,12,128,128]{3,2,1,0:T(8,128)(2,1)S(1)} %get-tuple-element.61), channel_id=1, source_target_pairs={{0,1},{1,0},{2,3},{3,2},{4,5},{5,4},{6,7},{7,6},{8,9},{9,8},{10,11... | collective-permute-start | bytes 4718600 | tf_op jit(solution)/shard_map/ppermute | solution.py:54
  83.8 7.6 %collective-permute-start.18 = (bf16[2,192,512]{2,1,0:T(8,128)(2,1)S(1)}, bf16[2,192,512]{2,1,0:T(8,128)(2,1)S(1)}, u32[]{:S(2)}, u32[]{:S(2)}) collective-permute-start(bf16[2,192,512]{2,1,0:T(8,128)(2,1)S(1)} %get-tuple-element.63), channel_id=1, source_target_pairs={{0,1},{1,0},{2,3},{3,2},{4,5},{5,4},{6,7},{7,6},{8,9},{9,8},{10,11... | collective-permute-start | bytes 1179656 | tf_op jit(solution)/shard_map/ppermute | solution.py:54
  87.1 4.4 %copy-start = (bf16[512,4096]{1,0:T(8,128)(2,1)S(1)}, bf16[512,4096]{1,0:T(8,128)(2,1)}, u32[]{:S(2)}) copy-start(bf16[512,4096]{1,0:T(8,128)(2,1)} %wo_any.1) | copy-start | bytes 12582916
  87.8 19.8 %collective-permute-start.21 = (bf16[12,128,128]{2,1,0:T(8,128)(2,1)S(1)}, bf16[12,128,128]{2,1,0:T(8,128)(2,1)S(1)}, u32[]{:S(2)}, u32[]{:S(2)}) collective-permute-start(bf16[12,128,128]{2,1,0:T(8,128)(2,1)S(1)} %get-tuple-element.79), channel_id=1, source_target_pairs={{0,6},{1,7},{2,0},{3,1},{4,2},{5,3},{6,4},{7,5},{8,14},{9,15},{10,... | collective-permute-start | bytes 1179656 | tf_op jit(solution)/shard_map/ppermute | solution.py:441
  90.5 17.1 %collective-permute-start.20 = (bf16[12,128,128]{2,1,0:T(8,128)(2,1)S(1)}, bf16[12,128,128]{2,1,0:T(8,128)(2,1)S(1)}, u32[]{:S(2)}, u32[]{:S(2)}) collective-permute-start(bf16[12,128,128]{2,1,0:T(8,128)(2,1)S(1)} %get-tuple-element.80), channel_id=1, source_target_pairs={{0,4},{1,5},{2,6},{3,7},{4,0},{5,1},{6,2},{7,3},{8,12},{9,13},{10,... | collective-permute-start | bytes 1179656 | tf_op jit(solution)/shard_map/ppermute | solution.py:441
  90.5 20.5 %collective-permute-start.19 = (bf16[12,128,128]{2,1,0:T(8,128)(2,1)S(1)}, bf16[12,128,128]{2,1,0:T(8,128)(2,1)S(1)}, u32[]{:S(2)}, u32[]{:S(2)}) collective-permute-start(bf16[12,128,128]{2,1,0:T(8,128)(2,1)S(1)} %get-tuple-element.81), channel_id=1, source_target_pairs={{0,2},{1,3},{2,4},{3,5},{4,6},{5,7},{6,0},{7,1},{8,10},{9,11},{10,... | collective-permute-start | bytes 1179656 | tf_op jit(solution)/shard_map/ppermute | solution.py:441
  111.0 37.5 %collective-permute-start.22 = (bf16[2,48,4096]{2,1,0:T(8,128)(2,1)}, bf16[2,48,4096]{2,1,0:T(8,128)(2,1)}, u32[]{:S(2)}, u32[]{:S(2)}) collective-permute-start(bf16[2,48,4096]{2,1,0:T(8,128)(2,1)} %get-tuple-element.69), channel_id=1, source_target_pairs={{0,2},{1,3},{2,4},{3,5},{4,6},{5,7},{6,0},{7,1},{8,10},{9,11},{10,... | collective-permute-start | bytes 2359304 | tf_op jit(solution)/shard_map/ppermute | solution.py:441
  111.0 37.5 %collective-permute-start.23 = (bf16[2,48,4096]{2,1,0:T(8,128)(2,1)}, bf16[2,48,4096]{2,1,0:T(8,128)(2,1)}, u32[]{:S(2)}, u32[]{:S(2)}) collective-permute-start(bf16[2,48,4096]{2,1,0:T(8,128)(2,1)} %get-tuple-element.70), channel_id=1, source_target_pairs={{0,4},{1,5},{2,6},{3,7},{4,0},{5,1},{6,2},{7,3},{8,12},{9,13},{10,... | collective-permute-start | bytes 2359304 | tf_op jit(solution)/shard_map/ppermute | solution.py:441
  113.4 35.8 %collective-permute-start.24 = (bf16[2,48,4096]{2,1,0:T(8,128)(2,1)S(1)}, bf16[2,48,4096]{2,1,0:T(8,128)(2,1)}, u32[]{:S(2)}, u32[]{:S(2)}) collective-permute-start(bf16[2,48,4096]{2,1,0:T(8,128)(2,1)S(1)} %get-tuple-element.71), channel_id=1, source_target_pairs={{0,6},{1,7},{2,0},{3,1},{4,2},{5,3},{6,4},{7,5},{8,14},{9,15},{10,... | collective-permute-start | bytes 2359304 | tf_op jit(solution)/shard_map/ppermute | solution.py:441
  116.0 36.9 %all-to-all-start.1 = ((bf16[32,128,128]{2,1,0:T(8,128)(2,1)}), bf16[32,128,128]{2,1,0:T(8,128)(2,1)S(1)}, u32[]{:S(2)}, u32[]{:S(2)}) async-start(bf16[32,128,128]{2,1,0:T(8,128)(2,1)} %place.1), calls=%async_computation.1 | async-start | bytes 2097152 | tf_op jit(solution)/shard_map/all_to_all | solution.py:486
